TPU v7x, 32 devices: a whole 2x2x4 slice. The times are simulated.
32 devices in a mesh: seq: 8 (over z, x), head: 4 (over y, core).
Axes of the slice: x: 2, y: 2, z: 4, core: 2. Of those that a mesh axis runs over, the one named last changes fastest.
Arguments:
- tokens: bfloat16 [2, 1024, 1024], P(None, 'seq', 'head'), may hold values from -6 to 6
- input_norm_gain: float32 [1024], replicated, may hold values from 0.1 to 1.9
- query_key_value_weight: bfloat16 [1024, 3, 1024], P(None, None, 'head'), may hold values from -0.1875 to 0.1875
- forget_gate_weight: bfloat16 [1024, 1024], P(None, 'head'), may hold values from -0.1875 to 0.1875
- convolution_filter_taps: float32 [2, 4, 3, 1024], P(None, None, None, 'head'), may hold values from -3 to 3
- slot_forget_rate: float32 [16, 64], P('head'), may hold values from 1.953125e-05 to 0.04
- extra_forget_log: float32 [2, 1024], P(None, 'seq'), may hold values from 0 to 1.4, as said below
- head_norm_gain: float32 [16, 64], P('head'), may hold values from 0.1 to 1.9
- output_projection_weight: bfloat16 [1024, 1024], P('head'), may hold values from -0.1875 to 0.1875
- feedforward_norm_gain: float32 [1024], replicated, may hold values from 0.1 to 1.9
- up_projection_weight: bfloat16 [1024, 4096], P(None, 'head'), may hold values from -0.1875 to 0.1875
- down_projection_weight: bfloat16 [4096, 1024], P('head'), may hold values from -0.09375 to 0.09375
Outputs:
- layer_out: bfloat16 [2, 1024, 1024], P(None, 'seq', 'head')
Inputs may be any that keep to these rules, and one draw needn't show every extreme that they name: `extra_forget_log`: one value per position of a sequence, zero at most positions.
All inputs are finite; a program needn't handle non-finite values.
Results may differ from a plain program's by a relative error of at most 0.01.
Values may be sent and summed in bfloat16 or wider, within the bound.
A program may use at most 128 MiB of HBM per device.

v0:
```python
import jax
import jax.numpy as jnp
from jax import lax
from jax.sharding import PartitionSpec as P

SPAN = 64


EPSILON = 1e-06
HIGHEST = lax.Precision.HIGHEST


def carried_in(value, axis, combine, identity, reverse):
    count, index = (lax.axis_size(axis), lax.axis_index(axis))
    everything = jax.tree.map(lambda part: lax.all_gather(part, axis), value)
    start = jax.tree.map(
        lambda part, zero: jnp.broadcast_to(jnp.asarray(zero, part.dtype), part.shape),
        value,
        identity,
    )

    def step(k, before):
        at = count - 1 - k if reverse else k
        reached = at > index if reverse else at < index
        new = combine(before, jax.tree.map(lambda part: part[at], everything))
        return jax.tree.map(lambda a, b: jnp.where(reached, a, b), new, before)

    return lax.fori_loop(0, count, step, start)


def with_halo(value, sides, width):
    for axis, dim in sides:
        count, length = (lax.axis_size(axis), value.shape[dim])
        up = [(i, (i + 1) % count) for i in range(count - 1)]
        down = [(j, i) for i, j in up]
        last = lax.slice_in_dim(value, length - width, length, axis=dim)
        first = lax.slice_in_dim(value, 0, width, axis=dim)
        before = lax.ppermute(last, axis, up)
        after = lax.ppermute(first, axis, down)
        value = jnp.concatenate([before, value, after], axis=dim)
    return value


def normalize(values, gain):
    return values * lax.rsqrt(jnp.mean(values * values, axis=-1, keepdims=True) + EPSILON) * gain


def convolve(padded, taps, backward):
    length = padded.shape[1] - 6
    running = jnp.zeros((padded.shape[0], length, padded.shape[2]), jnp.float32)
    for offset in range(4):
        first_row = 3 + offset if backward else 3 - offset
        running = running + taps[offset] * padded[:, first_row : first_row + length]
    return jax.nn.silu(running).astype(jnp.bfloat16)


def split_heads(mixed, head_count, head_size):
    grouped = mixed.astype(jnp.float32).reshape(
        mixed.shape[0], mixed.shape[1], 3, head_count, head_size
    )
    grouped = jnp.transpose(grouped, (2, 0, 3, 1, 4))
    return (grouped[0], grouped[1], grouped[2])


def log_decay_values(gate_scores, slot_forget_rate, extra_forget_log):
    head_count, slot_count = slot_forget_rate.shape
    gate_opening = jax.nn.sigmoid(
        gate_scores.reshape(gate_scores.shape[0], gate_scores.shape[1], head_count, slot_count)
    )
    log_decay_total = -2.0 * slot_forget_rate * gate_opening - extra_forget_log[:, :, None, None]
    return jnp.transpose(log_decay_total, (0, 2, 1, 3))


def flipped(array):
    return jnp.flip(array, axis=2)


def span_pass(state, block):
    queries, keys_in, values, log_decay_total = block
    state_key, state_value = state
    cumulative = jnp.cumsum(log_decay_total, axis=2)
    inflow = -jnp.expm1(log_decay_total)
    growth = jnp.exp(cumulative)
    shrink = jnp.exp(-cumulative) * inflow
    length = log_decay_total.shape[2]
    causal = (jnp.arange(length)[:, None] >= jnp.arange(length)[None, :]).astype(jnp.float32)
    intersection = jnp.einsum("bhtd,bhjd->bhtj", queries, keys_in, precision=HIGHEST) * causal
    scores = jnp.einsum("bhtj,bhjs->bhts", intersection, shrink, precision=HIGHEST)
    scores = growth * (
        scores + jnp.einsum("bhsd,bhtd->bhts", state_key, queries, precision=HIGHEST)
    )
    attend = jax.nn.softmax(scores, axis=-1)
    weighted = attend * growth
    mixing = jnp.einsum("bhts,bhjs->bhtj", weighted, shrink, precision=HIGHEST) * causal
    output = jnp.einsum("bhtj,bhjd->bhtd", mixing, values, precision=HIGHEST)
    output = output + jnp.einsum("bhts,bhsd->bhtd", weighted, state_value, precision=HIGHEST)
    ending = jnp.exp(cumulative[:, :, -1, :])
    remain = ending[:, :, None, :] * shrink
    state_key = ending[..., None] * state_key + jnp.einsum(
        "bhjs,bhjd->bhsd", remain, keys_in, precision=HIGHEST
    )
    state_value = ending[..., None] * state_value + jnp.einsum(
        "bhjs,bhjd->bhsd", remain, values, precision=HIGHEST
    )
    return ((state_key, state_value), output)


def recurrence(queries, keys_in, values, log_decay_total, state):
    batch_size, head_count, length = (queries.shape[0], queries.shape[1], queries.shape[2])
    blocks = length // SPAN

    def arrange(array):
        shaped = array.reshape(batch_size, head_count, blocks, SPAN, array.shape[3])
        return jnp.moveaxis(shaped, 2, 0)

    ignored, output = lax.scan(
        span_pass,
        state,
        (arrange(queries), arrange(keys_in), arrange(values), arrange(log_decay_total)),
    )
    return jnp.moveaxis(output, 0, 2).reshape(batch_size, head_count, length, output.shape[-1])


def summarize(keys_in, values, log_decay_total):
    cumulative = jnp.cumsum(log_decay_total, axis=2)
    totals = cumulative[:, :, -1, :]
    remain = jnp.exp(totals[:, :, None, :] - cumulative) * -jnp.expm1(log_decay_total)
    state_key = jnp.einsum("bhjs,bhjd->bhsd", remain, keys_in, precision=HIGHEST)
    state_value = jnp.einsum("bhjs,bhjd->bhsd", remain, values, precision=HIGHEST)
    return (totals, state_key, state_value)


def compose(earlier, latter):
    factor = jnp.exp(latter[0])[..., None]
    return (
        earlier[0] + latter[0],
        factor * earlier[1] + latter[1],
        factor * earlier[2] + latter[2],
    )


def forward_chain(summary):
    blank = (jnp.zeros_like(summary[0]), jnp.zeros_like(summary[1]), jnp.zeros_like(summary[2]))
    carried = carried_in((summary[0], summary[1], summary[2]), "seq", compose, blank, False)
    return (carried[1], carried[2])


def reverse_chain(summary):
    blank = (jnp.zeros_like(summary[0]), jnp.zeros_like(summary[1]), jnp.zeros_like(summary[2]))
    carried = carried_in((summary[0], summary[1], summary[2]), "seq", compose, blank, True)
    return (carried[1], carried[2])


def local(
    tokens,
    input_norm_gain,
    query_key_value_weight,
    forget_gate_weight,
    convolution_filter_taps,
    slot_forget_rate,
    extra_forget_log,
    head_norm_gain,
    output_projection_weight,
    feedforward_norm_gain,
    up_projection_weight,
    down_projection_weight,
):
    batch_size, row_count, part_width = tokens.shape
    head_count = slot_forget_rate.shape[0]
    head_size = head_norm_gain.shape[1]
    weight_flat = query_key_value_weight.reshape(query_key_value_weight.shape[0], -1)
    taps = convolution_filter_taps.reshape(2, 4, -1)
    extended = with_halo(tokens, (("seq", 1),), 3)
    gathered = lax.all_gather(extended, "head", axis=2, tiled=True)
    normed_all = normalize(gathered.astype(jnp.float32), input_norm_gain).astype(jnp.bfloat16)
    projected = jnp.dot(normed_all, weight_flat, preferred_element_type=jnp.float32).astype(
        jnp.bfloat16
    )
    padded = projected.astype(jnp.float32)
    normed = normed_all[:, 3 : 3 + row_count]
    gate_scores = jnp.dot(normed, forget_gate_weight, preferred_element_type=jnp.float32)
    log_decay_total = log_decay_values(gate_scores, slot_forget_rate, extra_forget_log)
    reverse_decay = flipped(log_decay_total)
    forward_parts = split_heads(convolve(padded, taps[0], False), head_count, head_size)
    reverse_parts = [
        flipped(member)
        for member in split_heads(convolve(padded, taps[1], True), head_count, head_size)
    ]
    forward_state = forward_chain(summarize(forward_parts[1], forward_parts[2], log_decay_total))
    forward_out = recurrence(
        forward_parts[0], forward_parts[1], forward_parts[2], log_decay_total, forward_state
    )
    reverse_state = reverse_chain(summarize(reverse_parts[1], reverse_parts[2], reverse_decay))
    reverse_out = recurrence(
        reverse_parts[0], reverse_parts[1], reverse_parts[2], reverse_decay, reverse_state
    )
    gain_shape = head_norm_gain[None, :, None, :]
    combined = normalize(forward_out, gain_shape) + normalize(flipped(reverse_out), gain_shape)
    attention = (
        jnp.transpose(combined, (0, 2, 1, 3))
        .reshape(batch_size, row_count, head_count * head_size)
        .astype(jnp.bfloat16)
    )
    partial_sum = jnp.dot(attention, output_projection_weight, preferred_element_type=jnp.float32)
    shared = lax.psum_scatter(partial_sum, "head", scatter_dimension=2, tiled=True)
    residual = (tokens.astype(jnp.float32) + shared).astype(jnp.bfloat16)
    resid_whole = lax.all_gather(residual, "head", axis=2, tiled=True)
    mlp_in = normalize(resid_whole.astype(jnp.float32), feedforward_norm_gain).astype(jnp.bfloat16)
    hidden = jax.nn.gelu(
        jnp.dot(mlp_in, up_projection_weight, preferred_element_type=jnp.float32)
    ).astype(jnp.bfloat16)
    terms = jnp.dot(hidden, down_projection_weight, preferred_element_type=jnp.float32)
    update = lax.psum_scatter(terms, "head", scatter_dimension=2, tiled=True)
    return (residual.astype(jnp.float32) + update).astype(jnp.bfloat16)


def solution(mesh):
    in_specs = (
        P(None, "seq", "head"),
        P(),
        P(None, None, "head"),
        P(None, "head"),
        P(None, None, None, "head"),
        P("head", None),
        P(None, "seq"),
        P("head", None),
        P("head", None),
        P(),
        P(None, "head"),
        P("head", None),
    )
    out_specs = P(None, "seq", "head")
    return jax.shard_map(local, mesh=mesh, in_specs=in_specs, out_specs=out_specs, check_vma=False)
```

profile of v0, /device:TPU:0, one launch (start us, length us, event | category | flops | bytes accessed | tf_op | source)
XLA Modules:
  0.0 351.1 jit_solution(8831344579503703099)
XLA Ops:
  7.4 4.8 %collective-permute-start = (bf16[2,3,256]{2,1,0:T(4,128)(2,1)S(1)}, bf16[2,3,256]{2,1,0:T(4,128)(2,1)S(1)}, u32[]{:S(2)}, u32[]{:S(2)}) collective-permute-start(bf16[2,3,256]{2,1,0:T(4,128)(2,1)S(1)} %get-tuple-element.557), channel_id=1, source_target_pairs={{0,4},{4,8},{8,12},{12,16},{16,20},{20,24},{24,28},{1,5},{5,9},{9,... | collective-permute-start | bytes 9224 | tf_op jit(solution)/shard_map/ppermute | solution.py:38
  15.2 2.6 copy.118
  18.0 7.4 %all_gather.36 = bf16[2,134,1024]{2,1,0:T(8,128)(2,1)S(1)} all-gather(bf16[2,134,256]{2,1,0:T(8,128)(2,1)S(1)} %pad_maximum_fusion), channel_id=1, replica_groups=mesh['seq'=8,'head'=4] {'head'}, dimensions={2}, use_global_device_ids=true | all-gather | bytes 686080 | tf_op jit(solution)/shard_map/all_gather | solution.py:174
  30.6 1.8 multiply_convert_fusion.1
  35.4 2.3 fusion.94
  37.8 2.3 fusion.93
  40.1 3.4 rev.16
  43.6 2.3 copy.131
  45.8 2.0 slice_bitcast_fusion
  48.5 1.8 fusion.95
  51.7 2.0 fusion.106
  53.7 2.1 reshape_squeeze.9
  55.8 2.1 copy.125
  57.8 2.1 reshape_squeeze.10
  59.9 2.1 copy.126
  63.1 2.0 copy.127
  65.1 1.9 copy.166
  69.3 1.8 rev.19
  71.1 2.1 reshape.185
  74.0 33.1 %all-gather = f32[16,4,1,64]{3,1,2,0:T(4,128)S(1)} all-gather(f32[2,4,1,64]{3,1,2,0:T(4,128)S(1)} %bitcast.313), channel_id=2, replica_groups=mesh['seq'=8,'head'=4] {'seq'}, dimensions={0}, use_global_device_ids=true | all-gather | bytes 18432 | tf_op jit(solution)/shard_map/all_gather | solution.py:15
  107.1 30.8 %all-gather.3 = f32[16,4,1,64]{3,1,2,0:T(4,128)S(1)} all-gather(f32[2,4,1,64]{3,1,2,0:T(4,128)S(1)} %bitcast.315), channel_id=5, replica_groups=mesh['seq'=8,'head'=4] {'seq'}, dimensions={0}, use_global_device_ids=true | all-gather | bytes 18432 | tf_op jit(solution)/shard_map/all_gather | solution.py:15
  137.8 2.9 fusion.96
  141.0 17.0 %while.64 = (s32[]{:T(128)}, f32[2,4,64,64]{3,2,1,0:T(8,128)}, f32[2,4,64,64]{3,2,1,0:T(8,128)}, s32[]{:T(128)}, f32[8,2,4,64]{3,2,1,0:T(4,128)S(1)}, /*index=5*...) while((s32[]{:T(128)}, f32[2,4,64,64]{3,2,1,0:T(8,128)}, ...), condition=%wide.region_3.4_spmd.clone, body=%wide.region_2.3_spmd.clone.sunk | while | flops 262148 | bytes 792697 | solution.py:28
  141.1 2.0 fusion.223
  143.0 2.1 fusion.223
  145.2 2.1 fusion.223
  147.3 2.1 fusion.223
  149.5 2.1 fusion.223
  151.6 2.1 fusion.223
  153.7 2.1 fusion.223
  155.9 2.1 fusion.223
  158.9 29.7 %while.62 = (s32[]{:T(128)}, f32[2,4,64,64]{3,2,1,0:T(8,128)}, f32[2,4,64,64]{3,2,1,0:T(8,128)}, f32[2,2,4,64,64]{4,3,2,1,0:T(8,128)}, f32[2,2,4,64,64]{4,3,2,1,...) while((s32[]{:T(128)}, f32[2,4,64,64]{3,2,1,0:T(8,128)}, ...), condition=%wide.region_8.9_spmd, body=%wide.region_4.8_spmd.sunk | while | flops 204054592 | bytes 11745009 | solution.py:116
  169.1 2.4 convolution_add_fusion.12
  171.5 2.2 convolution_add_fusion.13
  183.9 2.4 convolution_add_fusion.12
  186.3 2.2 convolution_add_fusion.13
  188.6 2.1 copy.128
  190.7 2.1 reshape.180
  193.1 45.8 %all-gather.15.cloned.1.call-done = f32[16,4,64,64]{3,2,1,0:T(8,128)} async-done(((f32[2,4,64,64]{3,2,1,0:T(8,128)}), f32[16,4,64,64]{3,2,1,0:T(8,128)}) %all-gather.15.cloned.1.call-update) | async-done | bytes 1048592 | tf_op jit(solution)/shard_map/all_gather | solution.py:15
  238.8 10.3 %while.65 = (s32[]{:T(128)}, f32[2,4,64,64]{3,2,1,0:T(8,128)S(1)}, f32[2,4,64,64]{3,2,1,0:T(8,128)S(1)}, s32[]{:T(128)}, f32[8,2,4,64]{3,2,1,0:T(4,128)S(1)}, /*...) while((s32[]{:T(128)}, f32[2,4,64,64]{3,2,1,0:T(8,128)S(1)}, ...), condition=%wide.region_12.13_spmd.clone, body=%wide.region_11.12_spmd.clone.sunk | while | flops 262152 | bytes 792759 | solution.py:28
  250.0 27.2 %while.63 = (s32[]{:T(128)}, f32[2,4,64,64]{3,2,1,0:T(8,128)S(1)}, f32[2,4,64,64]{3,2,1,0:T(8,128)S(1)}, f32[2,2,4,64,64]{4,3,2,1,0:T(8,128)}, f32[2,2,4,64,64]{...) while((s32[]{:T(128)}, f32[2,4,64,64]{3,2,1,0:T(8,128)S(1)}, ...), condition=%wide.region_17.18_spmd, body=%wide.region_13.17_spmd.sunk | while | flops 204054592 | bytes 11206949 | solution.py:116
  252.3 2.5 constant_dynamic-slice_fusion.6
  265.8 2.5 constant_dynamic-slice_fusion.6
  279.2 2.4 fusion.81
  281.7 23.5 %reduce-scatter.3.cloned.1.call-done = f32[2,128,256]{2,1,0:T(8,128)} async-done(((f32[2,128,1024]{2,1,0:T(8,128)}), f32[2,128,256]{2,1,0:T(8,128)}) %reduce-scatter.3.cloned.1.call-update) | async-done | bytes 262160 | tf_op jit(solution)/shard_map/reduce_scatter | solution.py:205
  306.1 6.8 %all_gather.47 = bf16[2,128,1024]{2,1,0:T(8,128)(2,1)S(1)} all-gather(bf16[2,128,256]{2,1,0:T(8,128)(2,1)S(1)} %add_convert_fusion.1), channel_id=1, replica_groups=mesh['seq'=8,'head'=4] {'head'}, dimensions={2}, use_global_device_ids=true | all-gather | bytes 655360 | tf_op jit(solution)/shard_map/all_gather | solution.py:207
  313.1 4.1 %fusion.44 = f32[2,128,1024]{2,1,0:T(8,128)} fusion(bf16[1024,1024]{1,0:T(8,128)(2,1)S(1)} %copy-done, bf16[1024,1024]{1,0:T(8,128)(2,1)} %param.30, bf16[2,128,1024]{2,1,0:T(8,128)(2,1)S(1)} %all_gather.47, f32[1024]{0:T(1024)S(1)} %copy-done.23, f32[2,128]{1,0:T(2,128)S(1)} %add_rsqrt_fusion.3), kind=kOutput, calls=%fused_computation.75 | convolution fusion | flops 1077149696 | bytes 5772288 | tf_op jit(solution)/shard_map/dot_general | solution.py:212
  317.2 25.4 %reduce-scatter.5.cloned.1.call-done = f32[2,128,256]{2,1,0:T(8,128)} async-done(((f32[2,128,1024]{2,1,0:T(8,128)}), f32[2,128,256]{2,1,0:T(8,128)}) %reduce-scatter.5.cloned.1.call-update) | async-done | bytes 262160 | tf_op jit(solution)/shard_map/reduce_scatter | solution.py:213
  (221 shorter events, 77.2 us)
Async XLA Ops:
  6.5 306.5 %copy-start = (bf16[1024,1024]{1,0:T(8,128)(2,1)S(1)}, bf16[1024,1024]{1,0:T(8,128)(2,1)}, u32[]{:S(2)}) copy-start(bf16[1024,1024]{1,0:T(8,128)(2,1)} %param.31) | copy-start | bytes 6291460
  6.5 11.4 %copy-start.17 = (bf16[2,128,256]{2,1,0:T(8,128)(2,1)S(1)}, bf16[2,128,256]{2,1,0:T(8,128)(2,1)}, u32[]{:S(2)}) copy-start(bf16[2,128,256]{2,1,0:T(8,128)(2,1)} %param.20) | copy-start | bytes 393220
  6.5 134.4 %all-gather.11.cloned.1.call-start = ((), (), s32[]{:S(2)}) async-start(), calls=%async_computation.4 | async-start | bytes 2359296 | tf_op jit(solution)/shard_map/all_gather | solution.py:15
  7.4 10.5 %collective-permute-start = (bf16[2,3,256]{2,1,0:T(4,128)(2,1)S(1)}, bf16[2,3,256]{2,1,0:T(4,128)(2,1)S(1)}, u32[]{:S(2)}, u32[]{:S(2)}) collective-permute-start(bf16[2,3,256]{2,1,0:T(4,128)(2,1)S(1)} %get-tuple-element.557), channel_id=1, source_target_pairs={{0,4},{4,8},{8,12},{12,16},{16,20},{20,24},{24,28},{1,5},{5,9},{9,... | collective-permute-start | bytes 9224 | tf_op jit(solution)/shard_map/ppermute | solution.py:38
  12.3 5.7 %collective-permute-start.1 = (bf16[2,3,256]{2,1,0:T(4,128)(2,1)S(1)}, bf16[2,3,256]{2,1,0:T(4,128)(2,1)S(1)}, u32[]{:S(2)}, u32[]{:S(2)}) collective-permute-start(bf16[2,3,256]{2,1,0:T(4,128)(2,1)S(1)} %get-tuple-element.558), channel_id=1, source_target_pairs={{4,0},{8,4},{12,8},{16,12},{20,16},{24,20},{28,24},{5,1},{9,5},{13... | collective-permute-start | bytes 9224 | tf_op jit(solution)/shard_map/ppermute | solution.py:39
  15.2 10.4 %copy-start.19 = (f32[1024]{0:T(1024)S(1)}, f32[1024]{0:T(1024)}, u32[]{:S(2)}) copy-start(f32[1024]{0:T(1024)} %param.21) | copy-start | bytes 12292
  17.8 8.8 %copy-start.22 = (bf16[1024,256]{1,0:T(8,128)(2,1)S(1)}, bf16[1024,256]{1,0:T(8,128)(2,1)}, u32[]{:S(2)}) copy-start(bf16[1024,256]{1,0:T(8,128)(2,1)} %param.23) | copy-start | bytes 1572868
  25.8 0.8 copy-start.13
  26.6 0.7 copy-start.20
  27.3 1.6 copy-start.8
  28.4 9.4 %copy-start.7 = (f32[2,128,4,64]{3,1,2,0:T(8,128)}, f32[2,128,4,64]{3,1,2,0:T(8,128)S(1)}, u32[]{:S(2)}) copy-start(f32[2,128,4,64]{3,1,2,0:T(8,128)S(1)} %multiply_subtract_fusion) | copy-start | bytes 786436
  37.7 103.3 %all-gather.13.cloned.1.call-start = ((), (), s32[]{:S(2)}) async-start(), calls=%async_computation.5 | async-start | bytes 2359296 | tf_op jit(solution)/shard_map/all_gather | solution.py:15
  40.1 153.0 %all-gather.17.cloned.1.call-start = ((), (), s32[]{:S(2)}) async-start(), calls=%async_computation.7 | async-start | bytes 2359296 | tf_op jit(solution)/shard_map/all_gather | solution.py:15
  48.5 2.0 copy-start.9
  50.4 188.5 %all-gather.15.cloned.1.call-start = ((), (), s32[]{:S(2)}) async-start(), calls=%async_computation.6 | async-start | bytes 2359296 | tf_op jit(solution)/shard_map/all_gather | solution.py:15
  140.7 164.4 %reduce-scatter.3.cloned.1.call-start = ((), (), s32[]{:S(2)}) async-start(), calls=%async_computation.2 | async-start | bytes 1310720 | tf_op jit(solution)/shard_map/reduce_scatter | solution.py:205
  164.2 2.8 copy-start.6
  164.2 3.2 copy-start.10
  166.0 3.0 copy-start.5
  169.0 2.5 copy-start.11
  179.1 2.8 copy-start.6
  179.1 3.2 copy-start.10
  180.8 3.1 copy-start.5
  183.9 2.5 copy-start.11
  188.6 4.2 %copy-start.12 = (f32[2,2,4,64,64]{4,3,2,1,0:T(8,128)S(1)}, f32[2,2,4,64,64]{4,3,2,1,0:T(8,128)}, u32[]{:S(2)}) copy-start(f32[2,2,4,64,64]{4,3,2,1,0:T(8,128)} %get-tuple-element.393) | copy-start | bytes 786436
  254.8 2.0 copy-start.1
  256.2 0.7 copy-start.2
  258.3 2.5 copy-start.4
  258.3 3.1 copy-start.14
  260.2 2.6 copy-start.3
  262.0 0.8 copy-start.15
  268.3 2.0 copy-start.1
  269.7 0.7 copy-start.2
  271.8 2.5 copy-start.4
  271.8 3.1 copy-start.14
  273.7 2.6 copy-start.3
  275.5 0.8 copy-start.15
  277.2 1.9 copy-start.16
  277.2 1.9 copy-start.21
  278.9 26.3 %copy-start.18 = (bf16[2,128,256]{2,1,0:T(8,128)(2,1)S(1)}, bf16[2,128,256]{2,1,0:T(8,128)(2,1)}, u32[]{:S(2)}) copy-start(bf16[2,128,256]{2,1,0:T(8,128)(2,1)} %param.20) | copy-start | bytes 393220
  279.2 33.9 %copy-start.23 = (f32[1024]{0:T(1024)S(1)}, f32[1024]{0:T(1024)}, u32[]{:S(2)}) copy-start(f32[1024]{0:T(1024)} %param.29) | copy-start | bytes 12292
  281.6 61.0 %reduce-scatter.5.cloned.1.call-start = ((), (), s32[]{:S(2)}) async-start(), calls=%async_computation.3 | async-start | bytes 1310720 | tf_op jit(solution)/shard_map/reduce_scatter | solution.py:213
Sparse Core Ops, SparseCore 0:
  37.8 51.0 all-gather.10
  91.0 47.9 all-gather.12
  141.2 47.8 all-gather.16
  191.0 47.7 all-gather.14
  281.7 23.3 reduce-scatter.2
  317.3 25.2 reduce-scatter.4
where the time goes:
time: 353 us; the launch traced here: 351 us
  waiting for transfers between devices  94.8 us (27%)
  blocking collectives  78 us (22%)
  local copies, waits for them, and re-layouts  58.3 us (17%)
  matrix products  54.4 us (15%)
  other arithmetic  44 us (12%)
  between operations  13.9 us (4%)
  starting transfers between devices  6.51 us (2%)
    all_gather x2, blocking collectives, carried_in(): everything = jax.tree.map(lambda part: lax.all_gather(part, axis), value)  63.9 us
    all_gather x4, waiting for transfers between devices, carried_in(): everything = jax.tree.map(lambda part: lax.all_gather(part, axis), value)  45.8 us
    select_n x16, other arithmetic, step(): return jax.tree.map(lambda a, b: jnp.where(reached, a, b), new, before)  26.8 us
    reduce_scatter x1, waiting for transfers between devices, local(): update = lax.psum_scatter(terms, 'head', scatter_dimension=2, tiled=True)  25.4 us
    reduce_scatter x1, waiting for transfers between devices, local(): lax.psum_scatter(partial_sum, 'head', scatter_dimension=2, tiled=True)  23.5 us
    another operation x6, local copies, waits for them, and re-layouts, arrange(): shaped = array.reshape(batch_size, head_count, blocks, SPAN, array.shape[3])  11.4 us
    dynamic_slice x4, local copies, waits for them, and re-layouts, recurrence(): lax.scan(span_pass, state, (arrange(queries), arrange(keys_in), arrange(v...  7.74 us
    all_gather x1, blocking collectives, local(): gathered = lax.all_gather(extended, 'head', axis=2, tiled=True)  7.38 us
  transfers between devices with their start and end apart: 8, of which 3 were waited for; matrix products, arithmetic and copies ran while one was open for 27% of the time, Pallas kernels for 0%

commit v1 on v0

v1 whole, which is shorter than its diff:
```python
import functools

import jax
import jax.numpy as jnp
from jax import lax
from jax.experimental import pallas as pl
from jax.experimental.pallas import tpu as pltpu
from jax.sharding import PartitionSpec as P

SPAN = 64
HALO = 16
EPSILON = 1e-06
MESH = pl.DeviceIdType.MESH
F32 = jnp.float32
BF16 = jnp.bfloat16


def mm(a, b, ca=1, cb=0):
    return lax.dot_general(a, b, (((ca,), (cb,)), ((), ())), preferred_element_type=F32)


def split_mm(ones, values, count):
    total, rest = None, values
    for _ in range(count):
        part = rest.astype(BF16)
        rest = rest - part.astype(F32)
        term = mm(ones, part)
        total = term if total is None else total + term
    return total


def mm_split(values, ones, count):
    total, rest = None, values
    for _ in range(count):
        part = rest.astype(BF16)
        rest = rest - part.astype(F32)
        term = mm(part, ones)
        total = term if total is None else total + term
    return total


def one_minus_exp(x):
    series = 1.0 + x * (1 / 2 + x * (1 / 6 + x * (1 / 24 + x * (1 / 120 + x * (1 / 720)))))
    return jnp.where(x > -0.25, -x * series, 1.0 - jnp.exp(x))


def iota(shape, dim):
    return lax.broadcasted_iota(jnp.int32, shape, dim)


class Gather:
    def __init__(self, hx, nh, seq, block, send, recv):
        self.hx, self.seq, self.block, self.send, self.recv = hx, seq, block, send, recv
        self.masks = []
        m = nh // 2
        while m:
            self.masks.append(m)
            m //= 2
        self.nh = nh
        self.got = {0}

    def copy(self, o, m):
        ref = self.block(self.hx(o))
        return pltpu.make_async_remote_copy(
            src_ref=ref,
            dst_ref=ref,
            send_sem=self.send.at[o ^ m],
            recv_sem=self.recv.at[o ^ m],
            device_id=(self.seq, self.hx(m)),
            device_id_type=MESH,
        )

    def arrive(self, o):
        if o not in self.got:
            ref = self.block(self.hx(o))
            pltpu.make_async_remote_copy(
                src_ref=ref,
                dst_ref=ref,
                send_sem=self.send.at[o],
                recv_sem=self.recv.at[o],
                device_id=(self.seq, self.hx(1)),
                device_id_type=MESH,
            ).wait_recv()
            self.got.add(o)

    def start(self):
        for m in self.masks:
            self.copy(0, m).start()

    def forward(self):
        have = [0]
        for m in self.masks:
            for o in have:
                if o:
                    self.arrive(o)
                    self.copy(o, m).start()
            have = have + [o ^ m for o in have]

    def finish(self):
        for o in range(1, self.nh):
            self.arrive(o)

    def drain(self):
        have = [0]
        for m in self.masks:
            for o in have:
                self.copy(o, m).wait_send()
            have = have + [o ^ m for o in have]


def kernel(
    n,
    nh,
    tok,
    gain1,
    wqkv,
    wgate,
    taps,
    rate,
    extra,
    hgain,
    wo,
    gain2,
    wup,
    wdown,
    out,
    xg,
    wq_v,
    wg_v,
    wo_v,
    up_v,
    dn_v,
    nb,
    pj,
    qkv,
    growth_v,
    shrink_v,
    score_v,
    local_v,
    before_v,
    apost,
    arecv,
    fpost,
    frecv,
    cin,
    csend,
    crecv,
    pair_v,
    pairf_v,
    ag,
    res,
    pf,
    pb,
    rb,
    lsem,
    tok_s,
    tok_r,
    halo_s,
    halo_r,
    wo_s,
    wo_r,
    sib_s,
    sib_r,
    ch_s,
    ch_r,
    at_s,
    at_r,
    rs_s,
    rs_r,
):
    batch, rows, width = tok.shape
    heads, hd = hgain.shape
    spans = rows // SPAN
    s = lax.axis_index("seq")
    h = lax.axis_index("head")

    def hx(o):
        r, bit = h, 1
        while bit <= o:
            if o & bit:
                r = r + bit - 2 * bit * lax.rem(lax.div(r, bit), 2)
            bit *= 2
        return r

    def ring(d):
        return lax.rem(s + d + n, n)

    odd = lax.rem(s, 2)
    pair = lax.div(s, 2)
    pairs = n // 2
    sibling = s + 1 - 2 * odd

    loads = [
        pltpu.make_async_copy(wqkv, wq_v, lsem.at[0]),
        pltpu.make_async_copy(wgate, wg_v, lsem.at[1]),
        pltpu.make_async_copy(wo, wo_v.at[h], lsem.at[2]),
        pltpu.make_async_copy(wup, up_v, lsem.at[3]),
        pltpu.make_async_copy(wdown, dn_v, lsem.at[4]),
    ]
    for load in loads:
        load.start()

    barrier = pltpu.get_barrier_semaphore()
    greeted = [(s, hx(1 << i)) for i in range(nh.bit_length() - 1)]
    greeted += [(ring(d), hx(o)) for d in (-1, 1) for o in range(nh)]
    greeted += [(ring(d), h) for d in (-2, 2)]
    for device in greeted:
        pl.semaphore_signal(barrier, inc=1, device_id=device, device_id_type=MESH)
    xg[h, :, HALO : HALO + rows, :] = tok[...]
    cin[...] = jnp.zeros_like(cin)
    pl.semaphore_wait(barrier, len(greeted))

    tokens = Gather(hx, nh, s, lambda i: xg.at[i, :, HALO : HALO + rows, :], tok_s, tok_r)
    tokens.start()
    halos = []
    for o in range(nh):
        for side in (0, 1):
            src = xg.at[h, :, rows : rows + HALO, :] if side == 0 else xg.at[h, :, HALO : 2 * HALO, :]
            at = 0 if side == 0 else HALO + rows
            halos.append(
                pltpu.make_async_remote_copy(
                    src_ref=src,
                    dst_ref=xg.at[h, :, at : at + HALO, :],
                    send_sem=halo_s.at[side, o],
                    recv_sem=halo_r.at[side, o],
                    device_id=(ring(1) if side == 0 else ring(-1), hx(o)),
                    device_id_type=MESH,
                )
            )
    for copy in halos:
        copy.start()
    tokens.forward()
    projection = Gather(hx, nh, s, lambda i: wo_v.at[i], wo_s, wo_r)
    loads[2].wait()
    projection.start()
    tokens.finish()
    for copy in halos:
        copy.wait_recv()

    tall = rows + 2 * HALO
    row_at = iota((tall, 1), 0)
    inside = jnp.logical_and(
        jnp.logical_or(row_at >= HALO, s > 0),
        jnp.logical_or(row_at < HALO + rows, s < n - 1),
    )
    for b in range(batch):
        parts = [xg[j, b].astype(F32) for j in range(nh)]
        square = parts[0] * parts[0]
        for part in parts[1:]:
            square = square + part * part
        mean = jnp.sum(square, axis=1, keepdims=True) / (nh * width)
        scale = jnp.where(inside, lax.rsqrt(mean + EPSILON), 0.0)
        for j in range(nh):
            cols = slice(j * width, (j + 1) * width)
            nb[b, :, cols] = (parts[j] * scale * gain1[:, cols]).astype(BF16)

    loads[0].wait()
    loads[1].wait()
    normed = nb[...].reshape(batch * tall, nh * width)
    for i in range(3):
        made = mm(normed, wq_v[i]).astype(BF16).astype(F32)
        pj[i] = made.reshape(batch, tall, width)

    lanes = iota((1, width), 1)
    lane_head = lax.div(lanes, hd)
    block_mask = (
        lax.div(iota((width, width), 0), hd) == lax.div(iota((width, width), 1), hd)
    ).astype(F32).astype(BF16)
    causal_t = iota((SPAN, width), 0)
    causal_j = lax.rem(iota((SPAN, width), 1), SPAN)
    causal = [(causal_t >= causal_j).astype(F32), (causal_t <= causal_j).astype(F32)]
    big_t, big_j = iota((rows, rows), 0), iota((rows, rows), 1)
    same = lax.div(big_t, SPAN) == lax.div(big_j, SPAN)
    running = [
        jnp.logical_and(same, big_t >= big_j).astype(F32).astype(BF16),
        jnp.logical_and(same, big_t <= big_j).astype(F32).astype(BF16),
    ]
    rate_row = jnp.concatenate([rate[i : i + 1, :] for i in range(heads)], axis=1)
    gain_row = jnp.concatenate([hgain[i : i + 1, :] for i in range(heads)], axis=1)

    def expand(x):
        return jnp.concatenate([x] * heads, axis=0) * block_mask

    def compact(x):
        total = None
        for i in range(heads):
            term = jnp.where(lane_head == i, x[i * hd : (i + 1) * hd], 0.0)
            total = term if total is None else total + term
        return total

    decays = []
    for b in range(batch):
        logits = mm(nb[b, HALO : HALO + rows, :], wg_v[...])
        column = jnp.sum(
            jnp.where(big_t == big_j, extra[b : b + 1, :], 0.0), axis=1, keepdims=True
        )
        decays.append(-2.0 * rate_row * jax.nn.sigmoid(logits) - column)

    def sib_copies(d):
        return [
            pltpu.make_async_remote_copy(
                src_ref=src.at[d],
                dst_ref=dst.at[d],
                send_sem=sib_s.at[d, k],
                recv_sem=sib_r.at[d, k],
                device_id=(sibling, h),
                device_id_type=MESH,
            )
            for k, (src, dst) in enumerate(((apost, arecv), (fpost, frecv)))
        ]

    fpost[...] = jnp.zeros_like(fpost)
    order = [list(range(spans)), list(range(spans))[::-1]]
    for d in (0, 1):
        for b in range(batch):
            for i in range(3):
                acc = None
                for j in range(4):
                    first = HALO + j if d else HALO - j
                    term = taps[d, i, j : j + 1, :] * pj[i, b, first : first + rows, :]
                    acc = term if acc is None else acc + term
                qkv[d, i, b] = (acc * jax.nn.sigmoid(acc)).astype(BF16)
            ld = decays[b]
            inflow = one_minus_exp(ld)
            cum = split_mm(running[d], ld, 3)
            growth_v[d, b] = jnp.exp(cum)
            shrink_v[d, b] = (jnp.exp(-cum) * inflow).astype(BF16)
            state = jnp.zeros((2 * hd, width), F32)
            past = jnp.zeros((1, width), F32)
            for g in order[d]:
                r0 = g * SPAN
                local_v[d, b, g] = state
                before_v[d, b, g : g + 1, :] = jnp.exp(past)
                last = r0 if d else r0 + SPAN - 1
                total = cum[last : last + 1, :]
                remain = (jnp.exp(total - cum[r0 : r0 + SPAN]) * inflow[r0 : r0 + SPAN]).astype(BF16)
                new = [
                    compact(mm(qkv[d, i, b, r0 : r0 + SPAN, :], remain, 0, 0)) for i in (1, 2)
                ]
                state = jnp.exp(total) * state + jnp.concatenate(new, axis=0)
                past = past + total
            apost[d, b] = state.astype(BF16)
            fpost[d, b : b + 1, :] = jnp.exp(past)
        for copy in sib_copies(d):
            copy.start()

    projection.forward()

    def local_scores(d):
        for b in range(batch):
            for g in range(spans):
                span = slice(g * SPAN, (g + 1) * SPAN)
                inter = mm(qkv[d, 0, b, span, :], expand(qkv[d, 1, b, span, :]), 1, 1) * causal[d]
                score_v[d, b, span, :] = mm(inter.astype(BF16), expand(shrink_v[d, b, span, :]))

    local_scores(0)

    later = [odd.astype(F32), 1.0 - odd.astype(F32)]
    for d in (0, 1):
        for copy in sib_copies(d):
            copy.wait_recv()
        for b in range(batch):
            mine, other = apost[d, b].astype(F32), arecv[d, b].astype(F32)
            fm, fo = fpost[d, b : b + 1, :], frecv[d, b : b + 1, :]
            pair_v[d, b] = later[d] * (fm * other + mine) + (1.0 - later[d]) * (fo * mine + other)
            pairf_v[d, b : b + 1, :] = fm * fo

    has_in = [pair > 0, pair < pairs - 1]
    has_out = [pair < pairs - 1, pair > 0]

    def hop_copy(d, b):
        return pltpu.make_async_remote_copy(
            src_ref=csend.at[d, b],
            dst_ref=crecv.at[d, b],
            send_sem=ch_s.at[d, b],
            recv_sem=ch_r.at[d, b],
            device_id=(ring(-2) if d else ring(2), h),
            device_id_type=MESH,
        )

    def hop(d):
        for b in range(batch):

            @pl.when(has_in[d])
            def _():
                hop_copy(d, b).wait_recv()
                cin[d, b] = crecv[d, b].astype(F32)

            @pl.when(has_out[d])
            def _():
                csend[d, b] = (pairf_v[d, b : b + 1, :] * cin[d, b] + pair_v[d, b]).astype(BF16)
                hop_copy(d, b).start()

    @pl.when(2 * pair < pairs)
    def _():
        hop(0)
        hop(1)

    @pl.when(2 * pair >= pairs)
    def _():
        hop(1)
        hop(0)

    local_scores(1)

    attends = [
        Gather(hx, nh, s, lambda i, b=b: ag.at[i, b], at_s.at[b], at_r.at[b]) for b in range(batch)
    ]
    for b in range(batch):
        for g in range(spans):
            span = slice(g * SPAN, (g + 1) * SPAN)
            combined = jnp.zeros((SPAN, width), F32)
            for d in (0, 1):
                fo = frecv[d, b : b + 1, :]
                carry = cin[d, b]
                entry = later[d] * (fo * carry + arecv[d, b].astype(F32)) + (1.0 - later[d]) * carry
                state = (before_v[d, b, g : g + 1, :] * entry + local_v[d, b, g]).astype(BF16)
                growth = growth_v[d, b, span, :]
                scores = score_v[d, b, span, :] + mm(qkv[d, 0, b, span, :], expand(state[:hd]))
                scores = growth * scores
                top = None
                for i in range(heads):
                    best = jnp.max(
                        jnp.where(lane_head == i, scores, -jnp.inf), axis=1, keepdims=True
                    )
                    top = best if top is None else jnp.where(lane_head == i, best, top)
                power = jnp.exp(scores - top)
                norm = mm_split(power, block_mask, 2)
                weighted = (power / norm * growth).astype(BF16)
                mixing = mm(weighted, expand(shrink_v[d, b, span, :]), 1, 1) * causal[d]
                made = mm(mixing.astype(BF16), expand(qkv[d, 2, b, span, :]))
                made = made + mm(weighted, expand(state[hd:]), 1, 1)
                mean = mm_split(made * made, block_mask, 2) / hd
                combined = combined + made * lax.rsqrt(mean + EPSILON) * gain_row
            ag[h, b, span, :] = combined.astype(BF16)
        attends[b].start()
        if b:
            attends[b - 1].forward()
    attends[batch - 1].forward()

    projection.finish()
    loads[3].wait()
    loads[4].wait()

    masks = [1 << i for i in range(nh.bit_length() - 1)]

    def rs_copy(b, o, m):
        return pltpu.make_async_remote_copy(
            src_ref=pb.at[hx(o), b],
            dst_ref=rb.at[o ^ m, m.bit_length() - 1, b],
            send_sem=rs_s.at[b, o],
            recv_sem=rs_r.at[b, o],
            device_id=(s, hx(m)),
            device_id_type=MESH,
        )

    def live(k):
        return [o for o in range(nh) if o % masks[k] == 0]

    def rs_send(b, k):
        m = masks[k]
        for o in live(k):
            if o & m:
                pb[hx(o), b] = pf[hx(o), b].astype(BF16)
                rs_copy(b, o, m).start()

    def rs_take(b, k):
        m = masks[k]
        for o in live(k):
            if o & m:
                rs_copy(b, o, m).wait_recv()
                kept = hx(o ^ m)
                pf[kept, b] = pf[kept, b] + rb[o ^ m, k, b].astype(F32)

    wo_all = wo_v[...].reshape(nh * width, nh * width)
    for b in range(batch):
        attends[b].finish()
        attention = jnp.concatenate([ag[j, b] for j in range(nh)], axis=1)
        whole = jnp.concatenate([xg[j, b, HALO : HALO + rows, :] for j in range(nh)], axis=1)
        residual = (whole.astype(F32) + mm(attention, wo_all)).astype(BF16)
        wide = residual.astype(F32)
        for j in range(nh):
            res[j, b] = residual[:, j * width : (j + 1) * width]
        mean = jnp.mean(wide * wide, axis=1, keepdims=True)
        mlp_in = (wide * lax.rsqrt(mean + EPSILON) * gain2[...]).astype(BF16)
        hidden = jax.nn.gelu(mm(mlp_in, up_v[...])).astype(BF16)
        for j in range(nh):
            pf[j, b] = mm(hidden, dn_v[:, j * width : (j + 1) * width])
        rs_send(b, 0)
    for k in range(len(masks)):
        for b in range(batch):
            rs_take(b, k)
            if k + 1 < len(masks):
                rs_send(b, k + 1)
    for b in range(batch):
        out[b] = (res[h, b].astype(F32) + pf[h, b]).astype(BF16)

    tokens.drain()
    projection.drain()
    for copy in halos:
        copy.wait_send()
    for d in (0, 1):
        for copy in sib_copies(d):
            copy.wait_send()

        @pl.when(has_out[d])
        def _():
            for b in range(batch):
                hop_copy(d, b).wait_send()

    for b in range(batch):
        attends[b].drain()
        for k, m in enumerate(masks):
            for o in live(k):
                if o & m:
                    rs_copy(b, o, m).wait_send()


def local(
    n,
    nh,
    tokens,
    input_norm_gain,
    query_key_value_weight,
    forget_gate_weight,
    convolution_filter_taps,
    slot_forget_rate,
    extra_forget_log,
    head_norm_gain,
    output_projection_weight,
    feedforward_norm_gain,
    up_projection_weight,
    down_projection_weight,
):
    batch, rows, width = tokens.shape
    depth = nh * width
    hidden = up_projection_weight.shape[1]
    spans = rows // SPAN
    hd = head_norm_gain.shape[1]
    tall = rows + 2 * HALO
    vmem = pl.BlockSpec(memory_space=pltpu.VMEM)
    anywhere = pl.BlockSpec(memory_space=pl.ANY)
    dma = pltpu.SemaphoreType.DMA
    bits = nh.bit_length() - 1
    scratch = [
        pltpu.VMEM((nh, batch, tall, width), BF16),
        pltpu.VMEM((3, depth, width), BF16),
        pltpu.VMEM((depth, width), BF16),
        pltpu.VMEM((nh, width, depth), BF16),
        pltpu.VMEM((depth, hidden), BF16),
        pltpu.VMEM((hidden, depth), BF16),
        pltpu.VMEM((batch, tall, depth), BF16),
        pltpu.VMEM((3, batch, tall, width), F32),
        pltpu.VMEM((2, 3, batch, rows, width), BF16),
        pltpu.VMEM((2, batch, rows, width), F32),
        pltpu.VMEM((2, batch, rows, width), BF16),
        pltpu.VMEM((2, batch, rows, width), F32),
        pltpu.VMEM((2, batch, spans, 2 * hd, width), F32),
        pltpu.VMEM((2, batch, spans, width), F32),
        pltpu.VMEM((2, batch, 2 * hd, width), BF16),
        pltpu.VMEM((2, batch, 2 * hd, width), BF16),
        pltpu.VMEM((2, 8 * pl.cdiv(batch, 8), width), F32),
        pltpu.VMEM((2, 8 * pl.cdiv(batch, 8), width), F32),
        pltpu.VMEM((2, batch, 2 * hd, width), F32),
        pltpu.VMEM((2, batch, 2 * hd, width), BF16),
        pltpu.VMEM((2, batch, 2 * hd, width), BF16),
        pltpu.VMEM((2, batch, 2 * hd, width), F32),
        pltpu.VMEM((2, batch, width), F32),
        pltpu.VMEM((nh, batch, rows, width), BF16),
        pltpu.VMEM((nh, batch, rows, width), BF16),
        pltpu.VMEM((nh, batch, rows, width), F32),
        pltpu.VMEM((nh, batch, rows, width), BF16),
        pltpu.VMEM((nh, bits, batch, rows, width), BF16),
        dma((5,)),
        dma((nh,)),
        dma((nh,)),
        dma((2, nh)),
        dma((2, nh)),
        dma((nh,)),
        dma((nh,)),
        dma((2, 2)),
        dma((2, 2)),
        dma((2, batch)),
        dma((2, batch)),
        dma((batch, nh)),
        dma((batch, nh)),
        dma((batch, nh)),
        dma((batch, nh)),
    ]
    return pl.pallas_call(
        functools.partial(kernel, n, nh),
        out_shape=jax.ShapeDtypeStruct(tokens.shape, tokens.dtype),
        in_specs=[
            vmem,
            vmem,
            anywhere,
            anywhere,
            vmem,
            vmem,
            vmem,
            vmem,
            anywhere,
            vmem,
            anywhere,
            anywhere,
        ],
        out_specs=vmem,
        scratch_shapes=scratch,
        compiler_params=pltpu.CompilerParams(
            collective_id=0, has_side_effects=True, vmem_limit_bytes=56 * 2**20
        ),
        name="layer",
    )(
        tokens,
        input_norm_gain.reshape(1, -1),
        jnp.transpose(query_key_value_weight, (1, 0, 2)),
        forget_gate_weight,
        jnp.transpose(convolution_filter_taps, (0, 2, 1, 3)),
        slot_forget_rate,
        extra_forget_log,
        head_norm_gain,
        output_projection_weight,
        feedforward_norm_gain.reshape(1, -1),
        up_projection_weight,
        down_projection_weight,
    )


def solution(mesh):
    in_specs = (
        P(None, "seq", "head"),
        P(),
        P(None, None, "head"),
        P(None, "head"),
        P(None, None, None, "head"),
        P("head", None),
        P(None, "seq"),
        P("head", None),
        P("head", None),
        P(),
        P(None, "head"),
        P("head", None),
    )
    out_specs = P(None, "seq", "head")
    return jax.shard_map(
        functools.partial(local, mesh.shape["seq"], mesh.shape["head"]),
        mesh=mesh,
        in_specs=in_specs,
        out_specs=out_specs,
        check_vma=False,
    )
```

time: 353 us -> 56.9 us (0.16)
  waiting for transfers between devices: 94.8 us -> 0 us
  blocking collectives: 78 us -> 0 us
  local copies, waits for them, and re-layouts: 58.3 us -> 1.57 us
  Pallas kernels: 0 us -> 55.2 us
  matrix products: 54.4 us -> 0 us
  other arithmetic: 44 us -> 0 us
  between operations: 13.9 us -> 0.01 us
  starting transfers between devices: 6.51 us -> 0 us
    all_gather x4 -> x0, blocking collectives: 78 us -> none  [the longest x2 63.9 us: carried_in(): everything = jax.tree.map(lambda part: lax.all_gather(part, axis), value)]
    pallas_call x0 -> x1, Pallas kernels: none -> 55.2 us  [local(): pl.pallas_call(functools.partial(kernel, n, nh), out_shape=jax.ShapeDtype...]
    dot_general x40 -> x0, matrix products: 54.4 us -> none  [the longest x4 6.45 us: span_pass(): jnp.einsum('bhsd,bhtd->bhts', state_key, queries, precision=HIGHEST)]
    reduce_scatter x2 -> x0, waiting for transfers between devices: 48.9 us -> none  [the longest x1 25.4 us: local(): update = lax.psum_scatter(terms, 'head', scatter_dimension=2, tiled=True)]
    all_gather x4 -> x0, waiting for transfers between devices: 45.8 us -> none  [carried_in(): everything = jax.tree.map(lambda part: lax.all_gather(part, axis), value)]
    select_n x16 -> x0, other arithmetic: 26.8 us -> none  [step(): return jax.tree.map(lambda a, b: jnp.where(reached, a, b), new, before)]
    another operation x12 -> x0, local copies, waits for them, and re-layouts: 13.6 us -> none  [the longest x6 11.4 us: arrange(): shaped = array.reshape(batch_size, head_count, blocks, SPAN, array.shape[3])]
    reshape x7 -> x0, local copies, waits for them, and re-layouts: 9.52 us -> none  [the longest x5 7.16 us: arrange(): shaped = array.reshape(batch_size, head_count, blocks, SPAN, array.shape[3])]
  transfers between devices with their start and end apart: 8 -> 0, of which waited for: 3 -> 0; matrix products, arithmetic and copies ran while one was open for 27% -> 0% of each run, Pallas kernels for 0% -> 0%
where the time goes in v1:
time: 56.9 us; the launch traced here: 56.8 us
  Pallas kernels  55.2 us (97%)
  local copies, waits for them, and re-layouts  1.57 us (3%)
    pallas_call x1, Pallas kernels, local(): pl.pallas_call(functools.partial(kernel, n, nh), out_shape=jax.ShapeDtype...  55.2 us
    unnamed x1, local copies, waits for them, and re-layouts  1.57 us

profile of v1, /device:TPU:0, one launch (start us, length us, event | category | flops | bytes accessed | tf_op | source)
XLA Modules:
  0.0 56.8 jit_solution(13316495482871639519)
XLA Ops:
  0.0 55.2 %layer.1 = bf16[2,128,256]{2,1,0:T(8,128)(2,1)} custom-call(bf16[2,128,256]{2,1,0:T(8,128)(2,1)} %tok.1, f32[1,1024]{1,0:T(1,128)} %bitcast.6, bf16[3,1024,256]{2,1,0:T(8,128)(2,1)} %bitcast.4, bf16[1024,256]{1,0:T(8,128)(2,1)} %wgate.1, f32[2,3,4,256]{3,2,1,0:T(4,128)} %bitcast.5, f32[4,64]{1,0:T(4,128)} %rate.1, f32[2,128]{1,0:T(2,128)} %extra.1, ...), custom_call_target="tpu_custom_call" | custom-call | tf_op jit(solution)/shard_map/layer/pallas_call | solution.py:590
  55.2 1.6 %copy.14 = bf16[2,128,256]{2,1,0:T(8,128)(2,1)} copy(bf16[2,128,256]{2,1,0:T(8,128)(2,1)} %layer.1) | data formatting | bytes 262144

commit v2 on v1

--- a/solution.py
+++ b/solution.py
@@ -145,6 +145,8 @@
     cin,
     csend,
     crecv,
+    sst,
+    begin,
     pair_v,
     pairf_v,
     ag,
@@ -163,6 +165,8 @@
     sib_r,
     ch_s,
     ch_r,
+    st_s,
+    st_r,
     at_s,
     at_r,
     rs_s,
@@ -257,9 +261,21 @@
     loads[0].wait()
     loads[1].wait()
     normed = nb[...].reshape(batch * tall, nh * width)
-    for i in range(3):
+
+    def project(i):
         made = mm(normed, wq_v[i]).astype(BF16).astype(F32)
         pj[i] = made.reshape(batch, tall, width)
+
+    def convolve(d, i, b):
+        acc = None
+        for j in range(4):
+            first = HALO + j if d else HALO - j
+            term = taps[d, i, j : j + 1, :] * pj[i, b, first : first + rows, :]
+            acc = term if acc is None else acc + term
+        qkv[d, i, b] = (acc * jax.nn.sigmoid(acc)).astype(BF16)
+
+    project(1)
+    project(2)
 
     lanes = iota((1, width), 1)
     lane_head = lax.div(lanes, hd)
@@ -299,27 +315,24 @@
     def sib_copies(d):
         return [
             pltpu.make_async_remote_copy(
-                src_ref=src.at[d],
-                dst_ref=dst.at[d],
+                src_ref=src,
+                dst_ref=dst,
                 send_sem=sib_s.at[d, k],
                 recv_sem=sib_r.at[d, k],
                 device_id=(sibling, h),
                 device_id_type=MESH,
             )
-            for k, (src, dst) in enumerate(((apost, arecv), (fpost, frecv)))
+            for k, (src, dst) in enumerate(
+                ((apost.at[d, 1 - odd], arecv.at[d]), (fpost.at[d], frecv.at[d]))
+            )
         ]
 
     fpost[...] = jnp.zeros_like(fpost)
     order = [list(range(spans)), list(range(spans))[::-1]]
     for d in (0, 1):
         for b in range(batch):
-            for i in range(3):
-                acc = None
-                for j in range(4):
-                    first = HALO + j if d else HALO - j
-                    term = taps[d, i, j : j + 1, :] * pj[i, b, first : first + rows, :]
-                    acc = term if acc is None else acc + term
-                qkv[d, i, b] = (acc * jax.nn.sigmoid(acc)).astype(BF16)
+            for i in (1, 2):
+                convolve(d, i, b)
             ld = decays[b]
             inflow = one_minus_exp(ld)
             cum = split_mm(running[d], ld, 3)
@@ -339,34 +352,39 @@
                 ]
                 state = jnp.exp(total) * state + jnp.concatenate(new, axis=0)
                 past = past + total
-            apost[d, b] = state.astype(BF16)
+            apost[d, 0, b] = state[:hd].astype(BF16)
+            apost[d, 1, b] = state[hd:].astype(BF16)
             fpost[d, b : b + 1, :] = jnp.exp(past)
         for copy in sib_copies(d):
             copy.start()
 
-    projection.forward()
+    project(0)
+    for d in (0, 1):
+        for b in range(batch):
+            convolve(d, 0, b)
 
     def local_scores(d):
-        for b in range(batch):
-            for g in range(spans):
-                span = slice(g * SPAN, (g + 1) * SPAN)
-                inter = mm(qkv[d, 0, b, span, :], expand(qkv[d, 1, b, span, :]), 1, 1) * causal[d]
-                score_v[d, b, span, :] = mm(inter.astype(BF16), expand(shrink_v[d, b, span, :]))
-
-    local_scores(0)
+        blocks = [(b, slice(g * SPAN, (g + 1) * SPAN)) for b in range(batch) for g in range(spans)]
+        inter = [
+            mm(qkv[d, 0, b, span, :], expand(qkv[d, 1, b, span, :]), 1, 1) for b, span in blocks
+        ]
+        inter = [(x * causal[d]).astype(BF16) for x in inter]
+        made = [mm(x, expand(shrink_v[d, b, span, :])) for x, (b, span) in zip(inter, blocks)]
+        for x, (b, span) in zip(made, blocks):
+            score_v[d, b, span, :] = x
 
     later = [odd.astype(F32), 1.0 - odd.astype(F32)]
     for d in (0, 1):
         for copy in sib_copies(d):
             copy.wait_recv()
         for b in range(batch):
-            mine, other = apost[d, b].astype(F32), arecv[d, b].astype(F32)
+            mine, other = apost[d, odd, b].astype(F32), arecv[d, b].astype(F32)
             fm, fo = fpost[d, b : b + 1, :], frecv[d, b : b + 1, :]
             pair_v[d, b] = later[d] * (fm * other + mine) + (1.0 - later[d]) * (fo * mine + other)
             pairf_v[d, b : b + 1, :] = fm * fo
 
-    has_in = [pair > 0, pair < pairs - 1]
-    has_out = [pair < pairs - 1, pair > 0]
+    first_pair = [pair == 0, pair == pairs - 1]
+    last_pair = [pair == pairs - 1, pair == 0]
 
     def hop_copy(d, b):
         return pltpu.make_async_remote_copy(
@@ -378,65 +396,136 @@
             device_id_type=MESH,
         )
 
+    def start_copy(d, b):
+        return pltpu.make_async_remote_copy(
+            src_ref=sst.at[d, b],
+            dst_ref=begin.at[d, odd, b],
+            send_sem=st_s.at[d, b],
+            recv_sem=st_r.at[d, b],
+            device_id=(sibling, h),
+            device_id_type=MESH,
+        )
+
+    def await_start(d, b):
+        pltpu.make_async_remote_copy(
+            src_ref=sst.at[d, b],
+            dst_ref=begin.at[d, 1 - odd, b],
+            send_sem=st_s.at[d, b],
+            recv_sem=st_r.at[d, b],
+            device_id=(sibling, h),
+            device_id_type=MESH,
+        ).wait_recv()
+
+    def pass_on(d, b):
+        csend[d, b] = (pairf_v[d, b : b + 1, :] * cin[d, b] + pair_v[d, b]).astype(BF16)
+        hop_copy(d, b).start()
+
+    def open_chain(d):
+        @pl.when(jnp.logical_and(first_pair[d], jnp.logical_not(last_pair[d])))
+        def _():
+            for b in range(batch):
+                pass_on(d, b)
+
     def hop(d):
         for b in range(batch):
 
-            @pl.when(has_in[d])
+            @pl.when(jnp.logical_not(first_pair[d]))
             def _():
                 hop_copy(d, b).wait_recv()
                 cin[d, b] = crecv[d, b].astype(F32)
 
-            @pl.when(has_out[d])
+            @pl.when(jnp.logical_not(jnp.logical_or(first_pair[d], last_pair[d])))
             def _():
-                csend[d, b] = (pairf_v[d, b : b + 1, :] * cin[d, b] + pair_v[d, b]).astype(BF16)
-                hop_copy(d, b).start()
-
-    @pl.when(2 * pair < pairs)
+                pass_on(d, b)
+
+            carry = cin[d, b]
+            fm, fo = fpost[d, b : b + 1, :], frecv[d, b : b + 1, :]
+            mine, other = apost[d, odd, b].astype(F32), arecv[d, b].astype(F32)
+            theirs = (1.0 - later[d]) * (fm * carry + mine) + later[d] * carry
+            sst[d, b] = theirs.astype(BF16)
+            start_copy(d, b).start()
+            own = later[d] * (fo * carry + other) + (1.0 - later[d]) * carry
+            begin[d, odd, b] = own.astype(BF16)
+
+    lower = 2 * pair < pairs
+    open_chain(0)
+    open_chain(1)
+    local_scores(0)
+
+    @pl.when(lower)
     def _():
         hop(0)
-        hop(1)
-
-    @pl.when(2 * pair >= pairs)
+
+    @pl.when(jnp.logical_not(lower))
     def _():
         hop(1)
+
+    local_scores(1)
+
+    @pl.when(lower)
+    def _():
+        hop(1)
+
+    @pl.when(jnp.logical_not(lower))
+    def _():
         hop(0)
 
-    local_scores(1)
+    projection.forward()
 
     attends = [
         Gather(hx, nh, s, lambda i, b=b: ag.at[i, b], at_s.at[b], at_r.at[b]) for b in range(batch)
     ]
+    group = min(width, 128)
+
+    def head_max(x):
+        tops = []
+        for c in range(0, width, group):
+            part, head = x[:, c : c + group], lane_head[:, c : c + group]
+            top = None
+            for i in range(c // hd, (c + group) // hd):
+                best = jnp.max(jnp.where(head == i, part, -jnp.inf), axis=1, keepdims=True)
+                top = best if top is None else jnp.where(head == i, best, top)
+            tops.append(jnp.broadcast_to(top, part.shape))
+        return jnp.concatenate(tops, axis=1)
+
     for b in range(batch):
+        for d in (0, 1):
+            await_start(d, b)
+        blocks = [(d, g, slice(g * SPAN, (g + 1) * SPAN)) for g in range(spans) for d in (0, 1)]
+        keys, values = [
+            [
+                (
+                    before_v[d, b, g : g + 1, :] * begin[d, i, b].astype(F32)
+                    + local_v[d, b, g, i * hd : (i + 1) * hd, :]
+                ).astype(BF16)
+                for d, g, span in blocks
+            ]
+            for i in (0, 1)
+        ]
+        growth = [growth_v[d, b, span, :] for d, g, span in blocks]
+        scores = [mm(qkv[d, 0, b, span, :], expand(k)) for (d, g, span), k in zip(blocks, keys)]
+        scores = [
+            w * (score_v[d, b, span, :] + x) for (d, g, span), x, w in zip(blocks, scores, growth)
+        ]
+        power = [jnp.exp(x - head_max(x)) for x in scores]
+        norm = [mm(x.astype(BF16), block_mask) for x in power]
+        weighted = [(x / y * w).astype(BF16) for x, y, w in zip(power, norm, growth)]
+        mixing = [
+            mm(x, expand(shrink_v[d, b, span, :]), 1, 1) for (d, g, span), x in zip(blocks, weighted)
+        ]
+        mixing = [(x * causal[d]).astype(BF16) for (d, g, span), x in zip(blocks, mixing)]
+        carried = [mm(x, expand(v), 1, 1) for x, v in zip(weighted, values)]
+        made = [
+            x + mm(y, expand(qkv[d, 2, b, span, :]))
+            for (d, g, span), x, y in zip(blocks, carried, mixing)
+        ]
+        mean = [mm((x * x).astype(BF16), block_mask) / hd for x in made]
+        made = [x * lax.rsqrt(y + EPSILON) * gain_row for x, y in zip(made, mean)]
         for g in range(spans):
             span = slice(g * SPAN, (g + 1) * SPAN)
-            combined = jnp.zeros((SPAN, width), F32)
-            for d in (0, 1):
-                fo = frecv[d, b : b + 1, :]
-                carry = cin[d, b]
-                entry = later[d] * (fo * carry + arecv[d, b].astype(F32)) + (1.0 - later[d]) * carry
-                state = (before_v[d, b, g : g + 1, :] * entry + local_v[d, b, g]).astype(BF16)
-                growth = growth_v[d, b, span, :]
-                scores = score_v[d, b, span, :] + mm(qkv[d, 0, b, span, :], expand(state[:hd]))
-                scores = growth * scores
-                top = None
-                for i in range(heads):
-                    best = jnp.max(
-                        jnp.where(lane_head == i, scores, -jnp.inf), axis=1, keepdims=True
-                    )
-                    top = best if top is None else jnp.where(lane_head == i, best, top)
-                power = jnp.exp(scores - top)
-                norm = mm_split(power, block_mask, 2)
-                weighted = (power / norm * growth).astype(BF16)
-                mixing = mm(weighted, expand(shrink_v[d, b, span, :]), 1, 1) * causal[d]
-                made = mm(mixing.astype(BF16), expand(qkv[d, 2, b, span, :]))
-                made = made + mm(weighted, expand(state[hd:]), 1, 1)
-                mean = mm_split(made * made, block_mask, 2) / hd
-                combined = combined + made * lax.rsqrt(mean + EPSILON) * gain_row
-            ag[h, b, span, :] = combined.astype(BF16)
+            ag[h, b, span, :] = (made[2 * g] + made[2 * g + 1]).astype(BF16)
         attends[b].start()
-        if b:
-            attends[b - 1].forward()
-    attends[batch - 1].forward()
+    attends[0].forward()
 
     projection.finish()
     loads[3].wait()
@@ -454,23 +543,21 @@
             device_id_type=MESH,
         )
 
-    def live(k):
-        return [o for o in range(nh) if o % masks[k] == 0]
-
-    def rs_send(b, k):
-        m = masks[k]
-        for o in live(k):
-            if o & m:
-                pb[hx(o), b] = pf[hx(o), b].astype(BF16)
-                rs_copy(b, o, m).start()
-
-    def rs_take(b, k):
-        m = masks[k]
-        for o in live(k):
-            if o & m:
-                rs_copy(b, o, m).wait_recv()
-                kept = hx(o ^ m)
-                pf[kept, b] = pf[kept, b] + rb[o ^ m, k, b].astype(F32)
+    leaving = sorted(range(nh), key=lambda o: [-((o >> k) & 1) for k in range(len(masks))])
+
+    def level(o):
+        return next((k for k, m in enumerate(masks) if o & m), len(masks))
+
+    def settle(b, o):
+        total = pf[hx(o), b]
+        for k in range(level(o)):
+            rs_copy(b, o ^ masks[k], masks[k]).wait_recv()
+            total = total + rb[o, k, b].astype(F32)
+        if o:
+            pb[hx(o), b] = total.astype(BF16)
+            rs_copy(b, o, masks[level(o)]).start()
+        else:
+            out[b] = (res[h, b].astype(F32) + total).astype(BF16)
 
     wo_all = wo_v[...].reshape(nh * width, nh * width)
     for b in range(batch):
@@ -484,16 +571,24 @@
         mean = jnp.mean(wide * wide, axis=1, keepdims=True)
         mlp_in = (wide * lax.rsqrt(mean + EPSILON) * gain2[...]).astype(BF16)
         hidden = jax.nn.gelu(mm(mlp_in, up_v[...])).astype(BF16)
-        for j in range(nh):
-            pf[j, b] = mm(hidden, dn_v[:, j * width : (j + 1) * width])
-        rs_send(b, 0)
-    for k in range(len(masks)):
-        for b in range(batch):
-            rs_take(b, k)
-            if k + 1 < len(masks):
-                rs_send(b, k + 1)
+        if b + 1 < batch:
+            attends[b + 1].forward()
+        if b:
+            for o in leaving:
+                if 0 < level(o) < len(masks):
+                    settle(b - 1, o)
+        for o in leaving:
+            cols = pl.ds(pl.multiple_of(hx(o) * width, width), width)
+            made = mm(hidden, dn_v[:, cols])
+            if level(o) == 0 and o:
+                pb[hx(o), b] = made.astype(BF16)
+                rs_copy(b, o, masks[0]).start()
+            else:
+                pf[hx(o), b] = made
+                if o and b == batch - 1:
+                    settle(b, o)
     for b in range(batch):
-        out[b] = (res[h, b].astype(F32) + pf[h, b]).astype(BF16)
+        settle(b, 0)
 
     tokens.drain()
     projection.drain()
@@ -503,17 +598,18 @@
         for copy in sib_copies(d):
             copy.wait_send()
 
-        @pl.when(has_out[d])
+        @pl.when(jnp.logical_not(last_pair[d]))
         def _():
             for b in range(batch):
                 hop_copy(d, b).wait_send()
 
+        for b in range(batch):
+            start_copy(d, b).wait_send()
+
     for b in range(batch):
         attends[b].drain()
-        for k, m in enumerate(masks):
-            for o in live(k):
-                if o & m:
-                    rs_copy(b, o, m).wait_send()
+        for o in range(1, nh):
+            rs_copy(b, o, masks[level(o)]).wait_send()
 
 
 def local(
@@ -557,14 +653,16 @@
         pltpu.VMEM((2, batch, rows, width), F32),
         pltpu.VMEM((2, batch, spans, 2 * hd, width), F32),
         pltpu.VMEM((2, batch, spans, width), F32),
-        pltpu.VMEM((2, batch, 2 * hd, width), BF16),
-        pltpu.VMEM((2, batch, 2 * hd, width), BF16),
+        pltpu.VMEM((2, 2, batch, hd, width), BF16),
+        pltpu.VMEM((2, batch, hd, width), BF16),
         pltpu.VMEM((2, 8 * pl.cdiv(batch, 8), width), F32),
         pltpu.VMEM((2, 8 * pl.cdiv(batch, 8), width), F32),
-        pltpu.VMEM((2, batch, 2 * hd, width), F32),
-        pltpu.VMEM((2, batch, 2 * hd, width), BF16),
-        pltpu.VMEM((2, batch, 2 * hd, width), BF16),
-        pltpu.VMEM((2, batch, 2 * hd, width), F32),
+        pltpu.VMEM((2, batch, hd, width), F32),
+        pltpu.VMEM((2, batch, hd, width), BF16),
+        pltpu.VMEM((2, batch, hd, width), BF16),
+        pltpu.VMEM((2, batch, hd, width), BF16),
+        pltpu.VMEM((2, 2, batch, hd, width), BF16),
+        pltpu.VMEM((2, batch, hd, width), F32),
         pltpu.VMEM((2, batch, width), F32),
         pltpu.VMEM((nh, batch, rows, width), BF16),
         pltpu.VMEM((nh, batch, rows, width), BF16),
@@ -580,6 +678,8 @@
         dma((nh,)),
         dma((2, 2)),
         dma((2, 2)),
+        dma((2, batch)),
+        dma((2, batch)),
         dma((2, batch)),
         dma((2, batch)),
         dma((batch, nh)),

time: 56.9 us -> 48.8 us (0.86)
  Pallas kernels: 55.2 us -> 47.1 us
    pallas_call x1, Pallas kernels: 55.2 us -> 47.1 us  [local(): pl.pallas_call(functools.partial(kernel, n, nh), out_shape=jax.ShapeDtype...]
where the time goes in v2:
time: 48.8 us; the launch traced here: 48.7 us
  Pallas kernels  47.1 us (97%)
  local copies, waits for them, and re-layouts  1.57 us (3%)
    pallas_call x1, Pallas kernels, local(): pl.pallas_call(functools.partial(kernel, n, nh), out_shape=jax.ShapeDtype...  47.1 us
    unnamed x1, local copies, waits for them, and re-layouts  1.57 us

profile of v2, /device:TPU:0, one launch (start us, length us, event | category | flops | bytes accessed | tf_op | source)
XLA Modules:
  0.0 48.7 jit_solution(7342641712141216009)
XLA Ops:
  0.0 47.1 %layer.1 = bf16[2,128,256]{2,1,0:T(8,128)(2,1)} custom-call(bf16[2,128,256]{2,1,0:T(8,128)(2,1)} %tok.1, f32[1,1024]{1,0:T(1,128)} %bitcast.6, bf16[3,1024,256]{2,1,0:T(8,128)(2,1)} %bitcast.4, bf16[1024,256]{1,0:T(8,128)(2,1)} %wgate.1, f32[2,3,4,256]{3,2,1,0:T(4,128)} %bitcast.5, f32[4,64]{1,0:T(4,128)} %rate.1, f32[2,128]{1,0:T(2,128)} %extra.1, ...), custom_call_target="tpu_custom_call" | custom-call | tf_op jit(solution)/shard_map/layer/pallas_call | solution.py:690
  47.1 1.6 %copy.14 = bf16[2,128,256]{2,1,0:T(8,128)(2,1)} copy(bf16[2,128,256]{2,1,0:T(8,128)(2,1)} %layer.1) | data formatting | bytes 262144

commit v3 on v2

--- a/solution.py
+++ b/solution.py
@@ -9,6 +9,7 @@
 
 SPAN = 64
 HALO = 16
+PIECES = 4
 EPSILON = 1e-06
 MESH = pl.DeviceIdType.MESH
 F32 = jnp.float32
@@ -49,8 +50,9 @@
 
 
 class Gather:
-    def __init__(self, hx, nh, seq, block, send, recv):
+    def __init__(self, hx, nh, seq, block, send, recv, direct=False):
         self.hx, self.seq, self.block, self.send, self.recv = hx, seq, block, send, recv
+        self.direct = direct
         self.masks = []
         m = nh // 2
         while m:
@@ -84,10 +86,12 @@
             self.got.add(o)
 
     def start(self):
-        for m in self.masks:
+        for m in range(1, self.nh) if self.direct else self.masks:
             self.copy(0, m).start()
 
     def forward(self):
+        if self.direct:
+            return
         have = [0]
         for m in self.masks:
             for o in have:
@@ -101,6 +105,10 @@
             self.arrive(o)
 
     def drain(self):
+        if self.direct:
+            for m in range(1, self.nh):
+                self.copy(0, m).wait_send()
+            return
         have = [0]
         for m in self.masks:
             for o in have:
@@ -205,7 +213,7 @@
         load.start()
 
     barrier = pltpu.get_barrier_semaphore()
-    greeted = [(s, hx(1 << i)) for i in range(nh.bit_length() - 1)]
+    greeted = [(s, hx(o)) for o in range(1, nh)]
     greeted += [(ring(d), hx(o)) for d in (-1, 1) for o in range(nh)]
     greeted += [(ring(d), h) for d in (-2, 2)]
     for device in greeted:
@@ -234,9 +242,16 @@
     for copy in halos:
         copy.start()
     tokens.forward()
-    projection = Gather(hx, nh, s, lambda i: wo_v.at[i], wo_s, wo_r)
+    piece = width // PIECES
+    projection = [
+        Gather(
+            hx, nh, s, lambda i, c=c: wo_v.at[i, c * piece : (c + 1) * piece, :], wo_s.at[c], wo_r.at[c]
+        )
+        for c in range(PIECES)
+    ]
     loads[2].wait()
-    projection.start()
+    projection[0].start()
+    projection[1].start()
     tokens.finish()
     for copy in halos:
         copy.wait_recv()
@@ -450,6 +465,7 @@
     lower = 2 * pair < pairs
     open_chain(0)
     open_chain(1)
+    projection[2].start()
     local_scores(0)
 
     @pl.when(lower)
@@ -460,6 +476,7 @@
     def _():
         hop(1)
 
+    projection[3].start()
     local_scores(1)
 
     @pl.when(lower)
@@ -470,10 +487,12 @@
     def _():
         hop(0)
 
-    projection.forward()
+    for member in projection[:2]:
+        member.forward()
 
     attends = [
-        Gather(hx, nh, s, lambda i, b=b: ag.at[i, b], at_s.at[b], at_r.at[b]) for b in range(batch)
+        Gather(hx, nh, s, lambda i, b=b: ag.at[i, b], at_s.at[b], at_r.at[b], b + 1 < batch)
+        for b in range(batch)
     ]
     group = min(width, 128)
 
@@ -525,9 +544,13 @@
             span = slice(g * SPAN, (g + 1) * SPAN)
             ag[h, b, span, :] = (made[2 * g] + made[2 * g + 1]).astype(BF16)
         attends[b].start()
+        if b == 0:
+            for member in projection[2:]:
+                member.forward()
     attends[0].forward()
 
-    projection.finish()
+    for member in projection:
+        member.finish()
     loads[3].wait()
     loads[4].wait()
 
@@ -591,7 +614,8 @@
         settle(b, 0)
 
     tokens.drain()
-    projection.drain()
+    for member in projection:
+        member.drain()
     for copy in halos:
         copy.wait_send()
     for d in (0, 1):
@@ -674,8 +698,8 @@
         dma((nh,)),
         dma((2, nh)),
         dma((2, nh)),
-        dma((nh,)),
-        dma((nh,)),
+        dma((PIECES, nh)),
+        dma((PIECES, nh)),
         dma((2, 2)),
         dma((2, 2)),
         dma((2, batch)),

time: 48.8 us -> 48.5 us (level)
  no operation moved by 1% of the time
where the time goes in v3:
time: 48.5 us; the launch traced here: 48.3 us
  Pallas kernels  46.8 us (96%)
  local copies, waits for them, and re-layouts  1.57 us (3%)
    pallas_call x1, Pallas kernels, local(): pl.pallas_call(functools.partial(kernel, n, nh), out_shape=jax.ShapeDtype...  46.8 us
    unnamed x1, local copies, waits for them, and re-layouts  1.57 us

profile of v3, /device:TPU:0, one launch (start us, length us, event | category | flops | bytes accessed | tf_op | source)
XLA Modules:
  0.0 48.3 jit_solution(7577603464517480491)
XLA Ops:
  0.0 46.8 %layer.1 = bf16[2,128,256]{2,1,0:T(8,128)(2,1)} custom-call(bf16[2,128,256]{2,1,0:T(8,128)(2,1)} %tok.1, f32[1,1024]{1,0:T(1,128)} %bitcast.6, bf16[3,1024,256]{2,1,0:T(8,128)(2,1)} %bitcast.4, bf16[1024,256]{1,0:T(8,128)(2,1)} %wgate.1, f32[2,3,4,256]{3,2,1,0:T(4,128)} %bitcast.5, f32[4,64]{1,0:T(4,128)} %rate.1, f32[2,128]{1,0:T(2,128)} %extra.1, ...), custom_call_target="tpu_custom_call" | custom-call | tf_op jit(solution)/shard_map/layer/pallas_call | solution.py:714
  46.8 1.6 %copy.14 = bf16[2,128,256]{2,1,0:T(8,128)(2,1)} copy(bf16[2,128,256]{2,1,0:T(8,128)(2,1)} %layer.1) | data formatting | bytes 262144

commit v4 on v3

--- a/solution.py
+++ b/solution.py
@@ -222,8 +222,13 @@
     cin[...] = jnp.zeros_like(cin)
     pl.semaphore_wait(barrier, len(greeted))
 
-    tokens = Gather(hx, nh, s, lambda i: xg.at[i, :, HALO : HALO + rows, :], tok_s, tok_r)
-    tokens.start()
+    tokens = [
+        Gather(
+            hx, nh, s, lambda i, b=b: xg.at[i, b, HALO : HALO + rows, :], tok_s.at[b], tok_r.at[b]
+        )
+        for b in range(batch)
+    ]
+    tokens[0].start()
     halos = []
     for o in range(nh):
         for side in (0, 1):
@@ -241,7 +246,9 @@
             )
     for copy in halos:
         copy.start()
-    tokens.forward()
+    for b in range(1, batch):
+        tokens[b].start()
+    tokens[0].forward()
     piece = width // PIECES
     projection = [
         Gather(
@@ -249,12 +256,10 @@
         )
         for c in range(PIECES)
     ]
-    loads[2].wait()
-    projection[0].start()
-    projection[1].start()
-    tokens.finish()
+    tokens[0].finish()
     for copy in halos:
         copy.wait_recv()
+    loads[2].wait()
 
     tall = rows + 2 * HALO
     row_at = iota((tall, 1), 0)
@@ -262,7 +267,7 @@
         jnp.logical_or(row_at >= HALO, s > 0),
         jnp.logical_or(row_at < HALO + rows, s < n - 1),
     )
-    for b in range(batch):
+    def norm_in(b):
         parts = [xg[j, b].astype(F32) for j in range(nh)]
         square = parts[0] * parts[0]
         for part in parts[1:]:
@@ -273,13 +278,8 @@
             cols = slice(j * width, (j + 1) * width)
             nb[b, :, cols] = (parts[j] * scale * gain1[:, cols]).astype(BF16)
 
-    loads[0].wait()
-    loads[1].wait()
-    normed = nb[...].reshape(batch * tall, nh * width)
-
-    def project(i):
-        made = mm(normed, wq_v[i]).astype(BF16).astype(F32)
-        pj[i] = made.reshape(batch, tall, width)
+    def project(i, b):
+        pj[i, b] = mm(nb[b], wq_v[i]).astype(BF16).astype(F32)
 
     def convolve(d, i, b):
         acc = None
@@ -288,9 +288,6 @@
             term = taps[d, i, j : j + 1, :] * pj[i, b, first : first + rows, :]
             acc = term if acc is None else acc + term
         qkv[d, i, b] = (acc * jax.nn.sigmoid(acc)).astype(BF16)
-
-    project(1)
-    project(2)
 
     lanes = iota((1, width), 1)
     lane_head = lax.div(lanes, hd)
@@ -319,37 +316,36 @@
             total = term if total is None else total + term
         return total
 
-    decays = []
-    for b in range(batch):
+    def decay(b):
         logits = mm(nb[b, HALO : HALO + rows, :], wg_v[...])
         column = jnp.sum(
             jnp.where(big_t == big_j, extra[b : b + 1, :], 0.0), axis=1, keepdims=True
         )
-        decays.append(-2.0 * rate_row * jax.nn.sigmoid(logits) - column)
-
-    def sib_copies(d):
+        return -2.0 * rate_row * jax.nn.sigmoid(logits) - column
+
+    def sib_copies(d, b):
         return [
             pltpu.make_async_remote_copy(
                 src_ref=src,
                 dst_ref=dst,
-                send_sem=sib_s.at[d, k],
-                recv_sem=sib_r.at[d, k],
+                send_sem=sib_s.at[d, b, k],
+                recv_sem=sib_r.at[d, b, k],
                 device_id=(sibling, h),
                 device_id_type=MESH,
             )
             for k, (src, dst) in enumerate(
-                ((apost.at[d, 1 - odd], arecv.at[d]), (fpost.at[d], frecv.at[d]))
+                ((apost.at[d, 1 - odd, b], arecv.at[d, b]), (fpost.at[d, b], frecv.at[d, b]))
             )
         ]
 
-    fpost[...] = jnp.zeros_like(fpost)
     order = [list(range(spans)), list(range(spans))[::-1]]
-    for d in (0, 1):
-        for b in range(batch):
+
+    def summarize(b):
+        ld = decay(b)
+        inflow = one_minus_exp(ld)
+        for d in (0, 1):
             for i in (1, 2):
                 convolve(d, i, b)
-            ld = decays[b]
-            inflow = one_minus_exp(ld)
             cum = split_mm(running[d], ld, 3)
             growth_v[d, b] = jnp.exp(cum)
             shrink_v[d, b] = (jnp.exp(-cum) * inflow).astype(BF16)
@@ -369,34 +365,34 @@
                 past = past + total
             apost[d, 0, b] = state[:hd].astype(BF16)
             apost[d, 1, b] = state[hd:].astype(BF16)
-            fpost[d, b : b + 1, :] = jnp.exp(past)
-        for copy in sib_copies(d):
-            copy.start()
-
-    project(0)
-    for d in (0, 1):
-        for b in range(batch):
+            fpost[d, b] = jnp.broadcast_to(jnp.exp(past), (8, width))
+            for copy in sib_copies(d, b):
+                copy.start()
+
+    def local_scores(b):
+        project(0, b)
+        for d in (0, 1):
             convolve(d, 0, b)
-
-    def local_scores(d):
-        blocks = [(b, slice(g * SPAN, (g + 1) * SPAN)) for b in range(batch) for g in range(spans)]
+        blocks = [(d, slice(g * SPAN, (g + 1) * SPAN)) for g in range(spans) for d in (0, 1)]
         inter = [
-            mm(qkv[d, 0, b, span, :], expand(qkv[d, 1, b, span, :]), 1, 1) for b, span in blocks
+            mm(qkv[d, 0, b, span, :], expand(qkv[d, 1, b, span, :]), 1, 1) for d, span in blocks
         ]
-        inter = [(x * causal[d]).astype(BF16) for x in inter]
-        made = [mm(x, expand(shrink_v[d, b, span, :])) for x, (b, span) in zip(inter, blocks)]
-        for x, (b, span) in zip(made, blocks):
+        inter = [(x * causal[d]).astype(BF16) for x, (d, span) in zip(inter, blocks)]
+        made = [mm(x, expand(shrink_v[d, b, span, :])) for x, (d, span) in zip(inter, blocks)]
+        for x, (d, span) in zip(made, blocks):
             score_v[d, b, span, :] = x
 
     later = [odd.astype(F32), 1.0 - odd.astype(F32)]
-    for d in (0, 1):
-        for copy in sib_copies(d):
-            copy.wait_recv()
-        for b in range(batch):
+
+    def join(b):
+        for d in (0, 1):
+            for copy in sib_copies(d, b):
+                copy.wait_recv()
             mine, other = apost[d, odd, b].astype(F32), arecv[d, b].astype(F32)
-            fm, fo = fpost[d, b : b + 1, :], frecv[d, b : b + 1, :]
+            fm, fo = fpost[d, b, :1, :], frecv[d, b, :1, :]
             pair_v[d, b] = later[d] * (fm * other + mine) + (1.0 - later[d]) * (fo * mine + other)
-            pairf_v[d, b : b + 1, :] = fm * fo
+            pairf_v[d, b] = jnp.broadcast_to(fm * fo, (8, width))
+            open_chain(d, b)
 
     first_pair = [pair == 0, pair == pairs - 1]
     last_pair = [pair == pairs - 1, pair == 0]
@@ -432,62 +428,79 @@
         ).wait_recv()
 
     def pass_on(d, b):
-        csend[d, b] = (pairf_v[d, b : b + 1, :] * cin[d, b] + pair_v[d, b]).astype(BF16)
+        csend[d, b] = (pairf_v[d, b, :1, :] * cin[d, b] + pair_v[d, b]).astype(BF16)
         hop_copy(d, b).start()
 
-    def open_chain(d):
+    def open_chain(d, b):
         @pl.when(jnp.logical_and(first_pair[d], jnp.logical_not(last_pair[d])))
         def _():
-            for b in range(batch):
-                pass_on(d, b)
-
-    def hop(d):
-        for b in range(batch):
-
-            @pl.when(jnp.logical_not(first_pair[d]))
-            def _():
-                hop_copy(d, b).wait_recv()
-                cin[d, b] = crecv[d, b].astype(F32)
-
-            @pl.when(jnp.logical_not(jnp.logical_or(first_pair[d], last_pair[d])))
-            def _():
-                pass_on(d, b)
-
-            carry = cin[d, b]
-            fm, fo = fpost[d, b : b + 1, :], frecv[d, b : b + 1, :]
-            mine, other = apost[d, odd, b].astype(F32), arecv[d, b].astype(F32)
-            theirs = (1.0 - later[d]) * (fm * carry + mine) + later[d] * carry
-            sst[d, b] = theirs.astype(BF16)
-            start_copy(d, b).start()
-            own = later[d] * (fo * carry + other) + (1.0 - later[d]) * carry
-            begin[d, odd, b] = own.astype(BF16)
+            pass_on(d, b)
+
+    def hop(d, b):
+        @pl.when(jnp.logical_not(first_pair[d]))
+        def _():
+            hop_copy(d, b).wait_recv()
+            cin[d, b] = crecv[d, b].astype(F32)
+
+        @pl.when(jnp.logical_not(jnp.logical_or(first_pair[d], last_pair[d])))
+        def _():
+            pass_on(d, b)
+
+        carry = cin[d, b]
+        fm, fo = fpost[d, b, :1, :], frecv[d, b, :1, :]
+        mine, other = apost[d, odd, b].astype(F32), arecv[d, b].astype(F32)
+        theirs = (1.0 - later[d]) * (fm * carry + mine) + later[d] * carry
+        sst[d, b] = theirs.astype(BF16)
+        start_copy(d, b).start()
+        own = later[d] * (fo * carry + other) + (1.0 - later[d]) * carry
+        begin[d, odd, b] = own.astype(BF16)
 
     lower = 2 * pair < pairs
-    open_chain(0)
-    open_chain(1)
-    projection[2].start()
-    local_scores(0)
-
-    @pl.when(lower)
-    def _():
-        hop(0)
-
-    @pl.when(jnp.logical_not(lower))
-    def _():
-        hop(1)
-
-    projection[3].start()
-    local_scores(1)
-
-    @pl.when(lower)
-    def _():
-        hop(1)
-
-    @pl.when(jnp.logical_not(lower))
-    def _():
-        hop(0)
-
-    for member in projection[:2]:
+    upper = jnp.logical_not(lower)
+
+    def near(b):
+        pl.when(lower)(lambda: hop(0, b))
+        pl.when(upper)(lambda: hop(1, b))
+
+    def far(b, ends):
+        for d, side in ((1, lower), (0, upper)):
+            end = last_pair[d] if ends else jnp.logical_not(last_pair[d])
+            pl.when(jnp.logical_and(side, end))(functools.partial(hop, d, b))
+
+    norm_in(0)
+    loads[0].wait()
+    loads[1].wait()
+    project(1, 0)
+    project(2, 0)
+    for b in range(1, batch):
+        tokens[b].forward()
+    projection[0].start()
+    summarize(0)
+    for b in range(1, batch):
+        tokens[b].finish()
+        norm_in(b)
+        project(1, b)
+        project(2, b)
+        join(b - 1)
+        projection[1].start() if b == 1 else None
+        summarize(b)
+    if batch == 1:
+        projection[1].start()
+    for b in range(batch):
+        if b:
+            near(b - 1)
+        if b == batch - 1:
+            join(b)
+        local_scores(b)
+        if b:
+            far(b - 1, False)
+            far(b - 1, True)
+        projection[2 + b].start() if b < 2 else None
+    near(batch - 1)
+    far(batch - 1, False)
+    if batch == 1:
+        projection[3].start()
+    for member in projection[:1]:
         member.forward()
 
     attends = [
@@ -507,7 +520,13 @@
             tops.append(jnp.broadcast_to(top, part.shape))
         return jnp.concatenate(tops, axis=1)
 
+    def stacked(xs):
+        sums = mm(jnp.concatenate([x.astype(BF16) for x in xs], axis=0), block_mask)
+        return [sums[i * SPAN : (i + 1) * SPAN] for i in range(len(xs))]
+
     for b in range(batch):
+        if b == batch - 1:
+            far(b, True)
         for d in (0, 1):
             await_start(d, b)
         blocks = [(d, g, slice(g * SPAN, (g + 1) * SPAN)) for g in range(spans) for d in (0, 1)]
@@ -527,7 +546,7 @@
             w * (score_v[d, b, span, :] + x) for (d, g, span), x, w in zip(blocks, scores, growth)
         ]
         power = [jnp.exp(x - head_max(x)) for x in scores]
-        norm = [mm(x.astype(BF16), block_mask) for x in power]
+        norm = stacked(power)
         weighted = [(x / y * w).astype(BF16) for x, y, w in zip(power, norm, growth)]
         mixing = [
             mm(x, expand(shrink_v[d, b, span, :]), 1, 1) for (d, g, span), x in zip(blocks, weighted)
@@ -538,14 +557,14 @@
             x + mm(y, expand(qkv[d, 2, b, span, :]))
             for (d, g, span), x, y in zip(blocks, carried, mixing)
         ]
-        mean = [mm((x * x).astype(BF16), block_mask) / hd for x in made]
+        mean = [x / hd for x in stacked([x * x for x in made])]
         made = [x * lax.rsqrt(y + EPSILON) * gain_row for x, y in zip(made, mean)]
         for g in range(spans):
             span = slice(g * SPAN, (g + 1) * SPAN)
             ag[h, b, span, :] = (made[2 * g] + made[2 * g + 1]).astype(BF16)
         attends[b].start()
         if b == 0:
-            for member in projection[2:]:
+            for member in projection[1:]:
                 member.forward()
     attends[0].forward()
 
@@ -613,14 +632,16 @@
     for b in range(batch):
         settle(b, 0)
 
-    tokens.drain()
+    for member in tokens:
+        member.drain()
     for member in projection:
         member.drain()
     for copy in halos:
         copy.wait_send()
     for d in (0, 1):
-        for copy in sib_copies(d):
-            copy.wait_send()
+        for b in range(batch):
+            for copy in sib_copies(d, b):
+                copy.wait_send()
 
         @pl.when(jnp.logical_not(last_pair[d]))
         def _():
@@ -679,29 +700,29 @@
         pltpu.VMEM((2, batch, spans, width), F32),
         pltpu.VMEM((2, 2, batch, hd, width), BF16),
         pltpu.VMEM((2, batch, hd, width), BF16),
-        pltpu.VMEM((2, 8 * pl.cdiv(batch, 8), width), F32),
-        pltpu.VMEM((2, 8 * pl.cdiv(batch, 8), width), F32),
+        pltpu.VMEM((2, batch, 8, width), F32),
+        pltpu.VMEM((2, batch, 8, width), F32),
         pltpu.VMEM((2, batch, hd, width), F32),
         pltpu.VMEM((2, batch, hd, width), BF16),
         pltpu.VMEM((2, batch, hd, width), BF16),
         pltpu.VMEM((2, batch, hd, width), BF16),
         pltpu.VMEM((2, 2, batch, hd, width), BF16),
         pltpu.VMEM((2, batch, hd, width), F32),
-        pltpu.VMEM((2, batch, width), F32),
+        pltpu.VMEM((2, batch, 8, width), F32),
         pltpu.VMEM((nh, batch, rows, width), BF16),
         pltpu.VMEM((nh, batch, rows, width), BF16),
         pltpu.VMEM((nh, batch, rows, width), F32),
         pltpu.VMEM((nh, batch, rows, width), BF16),
         pltpu.VMEM((nh, bits, batch, rows, width), BF16),
         dma((5,)),
-        dma((nh,)),
-        dma((nh,)),
+        dma((batch, nh)),
+        dma((batch, nh)),
         dma((2, nh)),
         dma((2, nh)),
         dma((PIECES, nh)),
         dma((PIECES, nh)),
-        dma((2, 2)),
-        dma((2, 2)),
+        dma((2, batch, 2)),
+        dma((2, batch, 2)),
         dma((2, batch)),
         dma((2, batch)),
         dma((2, batch)),

time: 48.5 us -> 49.3 us (1.016)
  Pallas kernels: 46.8 us -> 47.5 us
    pallas_call x1, Pallas kernels: 46.8 us -> 47.5 us  [local(): pl.pallas_call(functools.partial(kernel, n, nh), out_shape=jax.ShapeDtype...]
where the time goes in v4:
time: 49.3 us; the launch traced here: 49.1 us
  Pallas kernels  47.5 us (96%)
  local copies, waits for them, and re-layouts  1.57 us (3%)
    pallas_call x1, Pallas kernels, local(): pl.pallas_call(functools.partial(kernel, n, nh), out_shape=jax.ShapeDtype...  47.5 us
    unnamed x1, local copies, waits for them, and re-layouts  1.57 us

profile of v4, /device:TPU:0, one launch (start us, length us, event | category | flops | bytes accessed | tf_op | source)
XLA Modules:
  0.0 49.1 jit_solution(5203397651558204956)
XLA Ops:
  0.0 47.5 %layer.1 = bf16[2,128,256]{2,1,0:T(8,128)(2,1)} custom-call(bf16[2,128,256]{2,1,0:T(8,128)(2,1)} %tok.1, f32[1,1024]{1,0:T(1,128)} %bitcast.6, bf16[3,1024,256]{2,1,0:T(8,128)(2,1)} %bitcast.4, bf16[1024,256]{1,0:T(8,128)(2,1)} %wgate.1, f32[2,3,4,256]{3,2,1,0:T(4,128)} %bitcast.5, f32[4,64]{1,0:T(4,128)} %rate.1, f32[2,128]{1,0:T(2,128)} %extra.1, ...), custom_call_target="tpu_custom_call" | custom-call | tf_op jit(solution)/shard_map/layer/pallas_call | solution.py:735
  47.5 1.6 %copy.14 = bf16[2,128,256]{2,1,0:T(8,128)(2,1)} copy(bf16[2,128,256]{2,1,0:T(8,128)(2,1)} %layer.1) | data formatting | bytes 262144

commit v5 on v3

--- a/solution.py
+++ b/solution.py
@@ -302,10 +302,7 @@
     causal = [(causal_t >= causal_j).astype(F32), (causal_t <= causal_j).astype(F32)]
     big_t, big_j = iota((rows, rows), 0), iota((rows, rows), 1)
     same = lax.div(big_t, SPAN) == lax.div(big_j, SPAN)
-    running = [
-        jnp.logical_and(same, big_t >= big_j).astype(F32).astype(BF16),
-        jnp.logical_and(same, big_t <= big_j).astype(F32).astype(BF16),
-    ]
+    running = jnp.logical_and(same, big_t >= big_j).astype(F32).astype(BF16)
     rate_row = jnp.concatenate([rate[i : i + 1, :] for i in range(heads)], axis=1)
     gain_row = jnp.concatenate([hgain[i : i + 1, :] for i in range(heads)], axis=1)
 
@@ -326,6 +323,13 @@
             jnp.where(big_t == big_j, extra[b : b + 1, :], 0.0), axis=1, keepdims=True
         )
         decays.append(-2.0 * rate_row * jax.nn.sigmoid(logits) - column)
+    prefixes = split_mm(running, jnp.concatenate(decays, axis=1), 2)
+    prefixes = [prefixes[:, b * width : (b + 1) * width] for b in range(batch)]
+    inflows = [one_minus_exp(x) for x in decays]
+    totals = [
+        [prefixes[b][(g + 1) * SPAN - 1 : (g + 1) * SPAN] for g in range(spans)]
+        for b in range(batch)
+    ]
 
     def sib_copies(d):
         return [
@@ -344,29 +348,34 @@
 
     fpost[...] = jnp.zeros_like(fpost)
     order = [list(range(spans)), list(range(spans))[::-1]]
+    cells = [(b, g, slice(g * SPAN, (g + 1) * SPAN)) for b in range(batch) for g in range(spans)]
     for d in (0, 1):
+        remain = {}
+        for b, g, span in cells:
+            cum, ld = prefixes[b][span], decays[b][span]
+            if d:
+                cum = totals[b][g] - cum + ld
+            shrink = jnp.exp(-cum) * inflows[b][span]
+            growth_v[d, b, span, :] = jnp.exp(cum)
+            shrink_v[d, b, span, :] = shrink.astype(BF16)
+            remain[b, g] = (jnp.exp(totals[b][g]) * shrink).astype(BF16)
         for b in range(batch):
             for i in (1, 2):
                 convolve(d, i, b)
-            ld = decays[b]
-            inflow = one_minus_exp(ld)
-            cum = split_mm(running[d], ld, 3)
-            growth_v[d, b] = jnp.exp(cum)
-            shrink_v[d, b] = (jnp.exp(-cum) * inflow).astype(BF16)
+        fresh = {
+            (b, g, i): mm(qkv[d, i, b, span, :], remain[b, g], 0, 0)
+            for b, g, span in cells
+            for i in (1, 2)
+        }
+        for b in range(batch):
             state = jnp.zeros((2 * hd, width), F32)
             past = jnp.zeros((1, width), F32)
             for g in order[d]:
-                r0 = g * SPAN
                 local_v[d, b, g] = state
                 before_v[d, b, g : g + 1, :] = jnp.exp(past)
-                last = r0 if d else r0 + SPAN - 1
-                total = cum[last : last + 1, :]
-                remain = (jnp.exp(total - cum[r0 : r0 + SPAN]) * inflow[r0 : r0 + SPAN]).astype(BF16)
-                new = [
-                    compact(mm(qkv[d, i, b, r0 : r0 + SPAN, :], remain, 0, 0)) for i in (1, 2)
-                ]
-                state = jnp.exp(total) * state + jnp.concatenate(new, axis=0)
-                past = past + total
+                new = jnp.concatenate([compact(fresh[b, g, i]) for i in (1, 2)], axis=0)
+                state = jnp.exp(totals[b][g]) * state + new
+                past = past + totals[b][g]
             apost[d, 0, b] = state[:hd].astype(BF16)
             apost[d, 1, b] = state[hd:].astype(BF16)
             fpost[d, b : b + 1, :] = jnp.exp(past)
@@ -378,14 +387,14 @@
         for b in range(batch):
             convolve(d, 0, b)
 
-    def local_scores(d):
-        blocks = [(b, slice(g * SPAN, (g + 1) * SPAN)) for b in range(batch) for g in range(spans)]
+    def local_scores():
+        both = [(d, b, span) for d in (0, 1) for b, g, span in cells]
         inter = [
-            mm(qkv[d, 0, b, span, :], expand(qkv[d, 1, b, span, :]), 1, 1) for b, span in blocks
+            mm(qkv[d, 0, b, span, :], expand(qkv[d, 1, b, span, :]), 1, 1) for d, b, span in both
         ]
-        inter = [(x * causal[d]).astype(BF16) for x in inter]
-        made = [mm(x, expand(shrink_v[d, b, span, :])) for x, (b, span) in zip(inter, blocks)]
-        for x, (b, span) in zip(made, blocks):
+        inter = [(x * causal[d]).astype(BF16) for x, (d, b, span) in zip(inter, both)]
+        made = [mm(x, expand(shrink_v[d, b, span, :])) for x, (d, b, span) in zip(inter, both)]
+        for x, (d, b, span) in zip(made, both):
             score_v[d, b, span, :] = x
 
     later = [odd.astype(F32), 1.0 - odd.astype(F32)]
@@ -466,7 +475,7 @@
     open_chain(0)
     open_chain(1)
     projection[2].start()
-    local_scores(0)
+    local_scores()
 
     @pl.when(lower)
     def _():
@@ -477,7 +486,6 @@
         hop(1)
 
     projection[3].start()
-    local_scores(1)
 
     @pl.when(lower)
     def _():
@@ -506,6 +514,10 @@
                 top = best if top is None else jnp.where(head == i, best, top)
             tops.append(jnp.broadcast_to(top, part.shape))
         return jnp.concatenate(tops, axis=1)
+
+    def stacked(xs):
+        sums = mm(jnp.concatenate([x.astype(BF16) for x in xs], axis=0), block_mask)
+        return [sums[i * SPAN : (i + 1) * SPAN] for i in range(len(xs))]
 
     for b in range(batch):
         for d in (0, 1):
@@ -527,7 +539,7 @@
             w * (score_v[d, b, span, :] + x) for (d, g, span), x, w in zip(blocks, scores, growth)
         ]
         power = [jnp.exp(x - head_max(x)) for x in scores]
-        norm = [mm(x.astype(BF16), block_mask) for x in power]
+        norm = stacked(power)
         weighted = [(x / y * w).astype(BF16) for x, y, w in zip(power, norm, growth)]
         mixing = [
             mm(x, expand(shrink_v[d, b, span, :]), 1, 1) for (d, g, span), x in zip(blocks, weighted)
@@ -538,7 +550,7 @@
             x + mm(y, expand(qkv[d, 2, b, span, :]))
             for (d, g, span), x, y in zip(blocks, carried, mixing)
         ]
-        mean = [mm((x * x).astype(BF16), block_mask) / hd for x in made]
+        mean = [x / hd for x in stacked([x * x for x in made])]
         made = [x * lax.rsqrt(y + EPSILON) * gain_row for x, y in zip(made, mean)]
         for g in range(spans):
             span = slice(g * SPAN, (g + 1) * SPAN)

time: 48.5 us -> 48.3 us (level)
  no operation moved by 1% of the time
where the time goes in v5:
time: 48.3 us; the launch traced here: 48.1 us
  Pallas kernels  46.5 us (96%)
  local copies, waits for them, and re-layouts  1.57 us (3%)
    pallas_call x1, Pallas kernels, local(): pl.pallas_call(functools.partial(kernel, n, nh), out_shape=jax.ShapeDtype...  46.5 us
    unnamed x1, local copies, waits for them, and re-layouts  1.57 us

profile of v5, /device:TPU:0, one launch (start us, length us, event | category | flops | bytes accessed | tf_op | source)
XLA Modules:
  0.0 48.1 jit_solution(7149359646588907490)
XLA Ops:
  0.0 46.5 %layer.1 = bf16[2,128,256]{2,1,0:T(8,128)(2,1)} custom-call(bf16[2,128,256]{2,1,0:T(8,128)(2,1)} %tok.1, f32[1,1024]{1,0:T(1,128)} %bitcast.6, bf16[3,1024,256]{2,1,0:T(8,128)(2,1)} %bitcast.4, bf16[1024,256]{1,0:T(8,128)(2,1)} %wgate.1, f32[2,3,4,256]{3,2,1,0:T(4,128)} %bitcast.5, f32[4,64]{1,0:T(4,128)} %rate.1, f32[2,128]{1,0:T(2,128)} %extra.1, ...), custom_call_target="tpu_custom_call" | custom-call | tf_op jit(solution)/shard_map/layer/pallas_call | solution.py:726
  46.5 1.6 %copy.14 = bf16[2,128,256]{2,1,0:T(8,128)(2,1)} copy(bf16[2,128,256]{2,1,0:T(8,128)(2,1)} %layer.1) | data formatting | bytes 262144

commit v6 on v5

--- a/solution.py
+++ b/solution.py
@@ -382,11 +382,6 @@
         for copy in sib_copies(d):
             copy.start()
 
-    project(0)
-    for d in (0, 1):
-        for b in range(batch):
-            convolve(d, 0, b)
-
     def local_scores():
         both = [(d, b, span) for d in (0, 1) for b, g, span in cells]
         inter = [
@@ -398,7 +393,8 @@
             score_v[d, b, span, :] = x
 
     later = [odd.astype(F32), 1.0 - odd.astype(F32)]
-    for d in (0, 1):
+
+    def join(d):
         for copy in sib_copies(d):
             copy.wait_recv()
         for b in range(batch):
@@ -472,7 +468,13 @@
             begin[d, odd, b] = own.astype(BF16)
 
     lower = 2 * pair < pairs
+    join(0)
     open_chain(0)
+    project(0)
+    for d in (0, 1):
+        for b in range(batch):
+            convolve(d, 0, b)
+    join(1)
     open_chain(1)
     projection[2].start()
     local_scores()

time: 48.3 us -> 48.3 us (level)
  no operation moved by 1% of the time
where the time goes in v6:
time: 48.3 us; the launch traced here: 48.1 us
  Pallas kernels  46.5 us (96%)
  local copies, waits for them, and re-layouts  1.57 us (3%)
    pallas_call x1, Pallas kernels, local(): pl.pallas_call(functools.partial(kernel, n, nh), out_shape=jax.ShapeDtype...  46.5 us
    unnamed x1, local copies, waits for them, and re-layouts  1.57 us

profile of v6, /device:TPU:0, one launch (start us, length us, event | category | flops | bytes accessed | tf_op | source)
XLA Modules:
  0.0 48.1 jit_solution(14475032359357256018)
XLA Ops:
  0.0 46.5 %layer.1 = bf16[2,128,256]{2,1,0:T(8,128)(2,1)} custom-call(bf16[2,128,256]{2,1,0:T(8,128)(2,1)} %tok.1, f32[1,1024]{1,0:T(1,128)} %bitcast.6, bf16[3,1024,256]{2,1,0:T(8,128)(2,1)} %bitcast.4, bf16[1024,256]{1,0:T(8,128)(2,1)} %wgate.1, f32[2,3,4,256]{3,2,1,0:T(4,128)} %bitcast.5, f32[4,64]{1,0:T(4,128)} %rate.1, f32[2,128]{1,0:T(2,128)} %extra.1, ...), custom_call_target="tpu_custom_call" | custom-call | tf_op jit(solution)/shard_map/layer/pallas_call | solution.py:728
  46.5 1.6 %copy.14 = bf16[2,128,256]{2,1,0:T(8,128)(2,1)} copy(bf16[2,128,256]{2,1,0:T(8,128)(2,1)} %layer.1) | data formatting | bytes 262144
